TPU v7x, 512 devices: a whole 4x8x8 slice. The times are simulated.
512 devices in a mesh: dp: 32 (over y, z_hi), bal: 16 (over x, z_lo, core).
Axes of the slice: x: 4, y: 8, z: 8 (z_hi: 4, z_lo: 2; z = z_hi * 2 + z_lo), core: 2. Of those that a mesh axis runs over, the one named last changes fastest.
Arguments:
- counts: int32 [512], P(('dp', 'bal')), may hold values from 85 to 256, as said below
- rows: bfloat16 [131072, 1024], P(('dp', 'bal')), may hold values from -24 to 24
- cotangent: bfloat16 [131072, 512], P(('dp', 'bal')), may hold values from -6 to 6
- weight: bfloat16 [1024, 512], replicated, may hold values from -0.1875 to 0.1875
- gain: float32 [1024], replicated, may hold values from 0.1 to 1.9
- beta: float32 [1024], replicated, may hold values from -3 to 3
Outputs:
- grad_rows: bfloat16 [131072, 1024], P(('dp', 'bal'))
- grad_weight: float32 [1024, 512], P(('dp', 'bal'))
- grad_gain: float32 [1024], replicated
- grad_beta: float32 [1024], replicated
- grad_bias: float32 [512], replicated
Inputs may be any that keep to these rules, and one draw needn't show every extreme that they name: `counts`: some sample has exactly 256 visible rows.
All inputs are finite; a program needn't handle non-finite values.
Results may differ from a plain program's by a relative error of at most 0.0029.
Values may be sent and summed in bfloat16 or wider, within the bound.
No kernel may reach another device: no remote copies, remote signals or barrier semaphores. Data moves between devices by JAX's collectives and lax.ppermute only.
A program may use at most 64 MiB of HBM per device.

v0:
```python
import jax
import jax.numpy as jnp
from jax import lax
from jax.sharding import PartitionSpec as P

BLK_ROWS = 128
BLK_DEV = 2


epsilon = 1e-06


def row_grads(x_rows, cot_rows, live, gain, beta, weight):
    row_mask = (jnp.arange(x_rows.shape[0]) < live)[:, None]
    x_float = x_rows.astype(jnp.float32)
    centred = x_float - jnp.mean(x_float, axis=1, keepdims=True)
    inv_std = lax.rsqrt(jnp.mean(centred * centred, axis=1, keepdims=True) + epsilon)
    normed = centred * inv_std
    hidden = (normed * gain + beta).astype(jnp.bfloat16)
    hidden = jnp.where(row_mask, hidden, jnp.zeros_like(hidden))
    cot_live = jnp.where(row_mask, cot_rows, jnp.zeros_like(cot_rows))
    grad_w = lax.dot_general(
        hidden, cot_live, (((0,), (0,)), ((), ())), preferred_element_type=jnp.float32
    )
    grad_h = lax.dot_general(
        cot_live, weight, (((1,), (1,)), ((), ())), preferred_element_type=jnp.float32
    )
    grad_gain = jnp.sum(grad_h * normed, axis=0)
    grad_beta = jnp.sum(grad_h, axis=0)
    grad_bias = jnp.sum(cot_live.astype(jnp.float32), axis=0)
    scaled = grad_h * gain
    grad_x = inv_std * (
        scaled
        - jnp.mean(scaled, axis=1, keepdims=True)
        - normed * jnp.mean(scaled * normed, axis=1, keepdims=True)
    )
    grad_x = jnp.where(row_mask, grad_x, jnp.zeros_like(grad_x)).astype(jnp.bfloat16)
    return (grad_x, grad_w, grad_gain, grad_beta, grad_bias)


def body(counts, rows, cotangent, weight, gain, beta):
    width = rows.shape[1]
    decoder = cotangent.shape[1]
    block_rows = BLK_ROWS
    blocks = BLK_DEV
    my_count = counts[0]
    start_sums = (
        jnp.zeros((width, decoder), jnp.float32),
        jnp.zeros((width,), jnp.float32),
        jnp.zeros((width,), jnp.float32),
        jnp.zeros((decoder,), jnp.float32),
    )

    def add_block(sums, x_rows, cot_rows, live):
        grad_x, grad_w, grad_gain, grad_beta, grad_bias = row_grads(
            x_rows, cot_rows, live, gain, beta, weight
        )
        return (
            (sums[0] + grad_w, sums[1] + grad_gain, sums[2] + grad_beta, sums[3] + grad_bias),
            grad_x,
        )

    row_blocks = rows.reshape(blocks, block_rows, width)
    cot_blocks = cotangent.reshape(blocks, block_rows, decoder)
    own_blocks = (my_count + block_rows - 1) // block_rows

    def visit_own(turn, state):
        sums, grads = state
        sums, grad_x = add_block(
            sums, row_blocks[turn], cot_blocks[turn], my_count - turn * block_rows
        )
        return (sums, lax.dynamic_update_index_in_dim(grads, grad_x, turn, 0))

    empty_grads = jnp.zeros((blocks, block_rows, width), jnp.bfloat16)
    sums, grads = lax.fori_loop(0, own_blocks, visit_own, (start_sums, empty_grads))
    grad_rows = grads.reshape(blocks * block_rows, width)
    weight_local = sums[0]
    weight_sum = lax.psum_scatter(weight_local, ("dp", "bal"), scatter_dimension=0, tiled=True)
    total, gain_sum, beta_sum, bias_sum = lax.psum(
        (my_count.astype(jnp.float32), sums[1], sums[2], sums[3]), ("dp", "bal")
    )
    scale = lax.rsqrt(total)
    return (grad_rows, weight_sum * scale, gain_sum * scale, beta_sum * scale, bias_sum * scale)


def solution(mesh):
    placed = (P(("dp", "bal")), P(("dp", "bal"), None), P(("dp", "bal"), None), P(), P(), P())
    return jax.shard_map(
        body,
        mesh=mesh,
        in_specs=placed,
        out_specs=(P(("dp", "bal"), None), P(("dp", "bal"), None), P(), P(), P()),
        check_vma=False,
    )
```

profile of v0, /device:TPU:1, one launch (start us, length us, event | category | flops | bytes accessed | tf_op | source)
XLA Modules:
  0.0 311.5 jit_solution(133240916218483415)
XLA Ops:
  7.2 0.0 all-reduce.4.cloned.1.call-start
  8.0 0.2 broadcast_in_dim.47
  8.2 0.1 broadcast_in_dim.49
  8.4 7.9 %while.18 = (s32[]{:T(128)}, f32[1024,512]{1,0:T(8,128)S(1)}, f32[1024]{0:T(1024)S(1)}, f32[1024]{0:T(1024)S(1)}, f32[512]{0:T(512)S(1)}, /*index=5*/bf16[2,128,...) while((s32[]{:T(128)}, f32[1024,512]{1,0:T(8,128)S(1)}, ...), condition=%wide.region_8.9_spmd, body=%wide.region_0.8_spmd.sunk | while | flops 273613056 | bytes 8330219 | solution.py:75
  8.4 0.1 convert_reduce_fusion.4
  8.5 0.2 fusion.49
  9.4 1.9 fusion.50
  11.3 0.2 fusion.51
  11.6 0.6 convolution_add_fusion.2
  12.2 0.1 convert_reduce_fusion.5
  12.4 0.1 convert_reduce_fusion.4
  12.5 0.2 fusion.49
  13.4 1.8 fusion.50
  15.3 0.2 fusion.51
  15.5 0.6 convolution_add_fusion.2
  16.2 0.1 convert_reduce_fusion.5
  16.3 0.0 copy-start.3
  16.3 1.3 copy-done
  17.6 0.0 all-reduce.4.cloned.1.call-update
  17.6 106.5 %all-reduce.1 = (f32[]{:T(128)}, f32[1024]{0:T(1024)S(1)}, f32[1024]{0:T(1024)S(1)}, f32[512]{0:T(512)S(1)}) all-reduce(f32[]{:T(128)S(6)} %convert_element_type.20, f32[1024]{0:T(1024)S(1)} %get-tuple-element.79, f32[1024]{0:T(1024)S(1)} %get-tuple-element.80, ...), channel_id=1, replica_groups=mesh['dp'=32,'bal'=16] {'dp','bal'}, use_global_device_ids=true, to_apply=%region_10.11 | all-reduce | flops 2561 | bytes 20488 | tf_op jit(solution)/shard_map/psum | solution.py:79
  124.9 0.6 broadcast_multiply_fusion.5
  125.5 0.6 broadcast_multiply_fusion.3
  126.1 177.2 %all-reduce.4.cloned.1.call-done = f32[1024,512]{1,0:T(8,128)} async-done(((f32[1024,512]{1,0:T(8,128)}), f32[1024,512]{1,0:T(8,128)}) %all-reduce.4.cloned.1.call-update) | async-done | bytes 2097168
  303.3 1.3 dynamic-slice_multiply_fusion
  (27 shorter events, 0.1 us)
Async XLA Ops:
  7.2 1.2 copy-start.1
  7.2 1.2 copy-start.2
  7.2 1.2 copy-start.4
  7.2 1.2 copy-start.5
  7.2 296.1 %all-reduce.4.cloned.1.call-start = ((), (), s32[]{:S(2)}) async-start(), calls=%async_computation | async-start | bytes 4194304
  16.3 1.3 copy-start
  16.3 288.3 %copy-start.3 = (bf16[2,128,1024]{2,1,0:T(8,128)(2,1)}, bf16[2,128,1024]{2,1,0:T(8,128)(2,1)S(1)}, u32[]{:S(2)}) copy-start(bf16[2,128,1024]{2,1,0:T(8,128)(2,1)S(1)} %get-tuple-element.77) | copy-start | bytes 1572868
Sparse Core Ops, SparseCore 0:
  17.8 285.4 all-reduce.3
where the time goes:
time: 312 us; the launch traced here: 311 us
  waiting for transfers between devices  177 us (57%)
  blocking collectives  107 us (34%)
  between operations  15.6 us (5%)
  matrix products  4.97 us (2%)
  other arithmetic  3.97 us (1%)
    unnamed x2, waiting for transfers between devices  177 us
    psum x1, blocking collectives, body(): lax.psum((my_count.astype(jnp.float32), sums[1], sums[2], sums[3]), ('dp'...  107 us
  transfers between devices with their start and end apart: 1, of which 1 were waited for; matrix products, arithmetic and copies ran while one was open for 0% of the time, Pallas kernels for 0%

commit v1 on v0

v1 whole, which is shorter than its diff:
```python
import jax
import jax.numpy as jnp
from jax import lax
from jax.sharding import PartitionSpec as P

epsilon = 1e-06


def row_grads(x_rows, cot_rows, live, gain, beta, weight):
    row_mask = (jnp.arange(x_rows.shape[0]) < live)[:, None]
    x_float = x_rows.astype(jnp.float32)
    centred = x_float - jnp.mean(x_float, axis=1, keepdims=True)
    inv_std = lax.rsqrt(jnp.mean(centred * centred, axis=1, keepdims=True) + epsilon)
    normed = centred * inv_std
    hidden = (normed * gain + beta).astype(jnp.bfloat16)
    hidden = jnp.where(row_mask, hidden, jnp.zeros_like(hidden))
    cot_live = jnp.where(row_mask, cot_rows, jnp.zeros_like(cot_rows))
    grad_w = lax.dot_general(
        hidden, cot_live, (((0,), (0,)), ((), ())), preferred_element_type=jnp.float32
    )
    grad_h = lax.dot_general(
        cot_live, weight, (((1,), (1,)), ((), ())), preferred_element_type=jnp.float32
    )
    grad_gain = jnp.sum(grad_h * normed, axis=0)
    grad_beta = jnp.sum(grad_h, axis=0)
    grad_bias = jnp.sum(cot_live.astype(jnp.float32), axis=0)
    scaled = grad_h * gain
    grad_x = inv_std * (
        scaled
        - jnp.mean(scaled, axis=1, keepdims=True)
        - normed * jnp.mean(scaled * normed, axis=1, keepdims=True)
    )
    grad_x = jnp.where(row_mask, grad_x, jnp.zeros_like(grad_x)).astype(jnp.bfloat16)
    return (grad_x, grad_w, grad_gain, grad_beta, grad_bias)


def count_row(count, width):
    high = count // 256
    low = count - high * 256
    lane = jnp.arange(width)
    return jnp.where(lane == 0, high, jnp.where(lane == 1, low, 0)).astype(jnp.float32)[None, :]


def make_body(dp, bal):
    def body(counts, rows, cotangent, weight, gain, beta):
        width = rows.shape[1]
        decoder = cotangent.shape[1]
        own = width // (dp * bal)
        per_vector = width // decoder
        my_count = counts[0]
        grad_rows, grad_w, grad_gain, grad_beta, grad_bias = row_grads(
            rows, cotangent, my_count, gain, beta, weight
        )

        def pad_rows(small):
            return jnp.pad(small, ((0, -small.shape[0] % 8), (0, 0)))

        small = pad_rows(
            jnp.concatenate(
                [
                    grad_gain.reshape(per_vector, decoder),
                    grad_beta.reshape(per_vector, decoder),
                    grad_bias[None, :],
                    count_row(my_count, decoder),
                ]
            )
        )
        blocks = grad_w.reshape(dp, bal, own, decoder).transpose(1, 0, 2, 3)
        blocks = blocks.reshape(bal, dp * own, decoder)
        first = jnp.concatenate(
            [blocks, jnp.broadcast_to(small[None], (bal,) + small.shape)], axis=1
        ).astype(jnp.bfloat16)
        first = lax.all_to_all(first, "bal", 0, 0, tiled=True)
        first = jnp.sum(first.astype(jnp.float32), axis=0)
        part = first[: dp * own].reshape(dp, own, decoder)
        small = first[dp * own :]
        at = 2 * per_vector + 1
        count = small[at, 0].astype(jnp.int32) * 256 + small[at, 1].astype(jnp.int32)
        small = jnp.concatenate([small[:at], count_row(count, decoder)])
        second = jnp.concatenate(
            [part, jnp.broadcast_to(small[None], (dp,) + small.shape)], axis=1
        ).astype(jnp.bfloat16)
        second = lax.all_to_all(second, "dp", 0, 0, tiled=True)
        second = jnp.sum(second.astype(jnp.float32), axis=0)
        at = own + 2 * per_vector
        total = second[at + 1, 0] * 256.0 + second[at + 1, 1]
        second = second[: at + 1] * lax.rsqrt(total)
        return (
            grad_rows,
            second[:own],
            second[own : own + per_vector].reshape(width),
            second[own + per_vector : at].reshape(width),
            second[at],
        )

    return body


def solution(mesh):
    placed = (P(("dp", "bal")), P(("dp", "bal"), None), P(("dp", "bal"), None), P(), P(), P())
    return jax.shard_map(
        make_body(mesh.shape["dp"], mesh.shape["bal"]),
        mesh=mesh,
        in_specs=placed,
        out_specs=(P(("dp", "bal"), None), P(("dp", "bal"), None), P(), P(), P()),
        check_vma=False,
    )
```

time: 312 us -> 71.6 us (0.23)
  the two profiles are of different devices: /device:TPU:1 before, /device:TPU:8 now
where the time goes in v1:
time: 71.6 us; the launch traced here: 71.3 us
  blocking collectives  24 us (34%)
  starting transfers between devices  15.3 us (21%)
  waiting for transfers between devices  13.3 us (19%)
  local copies, waits for them, and re-layouts  7 us (10%)
  other arithmetic  5.08 us (7%)
  between operations  4.36 us (6%)
  matrix products  2.27 us (3%)
    all_to_all x1, blocking collectives, body(): first = lax.all_to_all(first, 'bal', 0, 0, tiled=True)  24 us
    all_to_all x1, starting transfers between devices, body(): second = lax.all_to_all(second, 'dp', 0, 0, tiled=True)  15.3 us
    all_to_all x1, waiting for transfers between devices, body(): second = lax.all_to_all(second, 'dp', 0, 0, tiled=True)  13.3 us
    reshape x2, local copies, waits for them, and re-layouts, body(): blocks = grad_w.reshape(dp, bal, own, decoder).transpose(1, 0, 2, 3)  2.69 us
    unnamed x15, local copies, waits for them, and re-layouts  1.81 us
    dot_general x1, matrix products, row_grads(): lax.dot_general(cot_live, weight, (((1,), (1,)), ((), ())), preferred_ele...  1.6 us
  transfers between devices with their start and end apart: 1, of which 1 were waited for; matrix products, arithmetic and copies ran while one was open for 2% of the time, Pallas kernels for 0%

profile of v1, /device:TPU:8, one launch (start us, length us, event | category | flops | bytes accessed | tf_op | source)
XLA Modules:
  0.0 71.3 jit_solution(1829162003108195419)
XLA Ops:
  0.6 0.0 copy-start
  0.6 0.0 copy-start.1
  1.5 1.2 %convert_reduce_fusion.1 = f32[256]{0:T(256)S(1)} fusion(bf16[256,1024]{1,0:T(8,128)(2,1)} %param.7), kind=kLoop, calls=%fused_computation.3 | loop fusion | flops 524032 | bytes 525312 | tf_op jit(solution)/shard_map/reduce_sum | solution.py:12
  2.7 1.3 %fusion.14 = f32[256]{0:T(256)S(1)} fusion(bf16[256,1024]{1,0:T(8,128)(2,1)} %param.7, f32[256]{0:T(256)S(1)} %broadcast_multiply_fusion.2), kind=kLoop, calls=%fused_computation.19 | loop fusion | flops 1048320 | bytes 526336 | tf_op jit(solution)/shard_map/reduce_sum | solution.py:13
  4.1 0.0 copy-done.3
  4.1 0.1 convert_reduce_fusion.3
  4.2 0.7 convolution_convert_fusion
  4.9 1.2 %reshape.103 = bf16[32,16,2,512]{3,2,1,0:T(2,128)(2,1)} reshape(bf16[1024,512]{1,0:T(8,128)(2,1)S(1)} %convolution_convert_fusion) | data formatting | bytes 2097152 | tf_op jit(solution)/shard_map/reshape | solution.py:68
  6.2 1.4 %copy.14 = bf16[32,16,2,512]{3,1,2,0:T(8,128)(2,1)S(1)} copy(bf16[32,16,2,512]{3,2,1,0:T(2,128)(2,1)} %reshape.103) | data formatting | bytes 2097152 | tf_op jit(solution)/shard_map/reshape | solution.py:68
  7.6 1.6 %fusion.13 = (bf16[1024]{0:T(1024)(128)(2,1)S(1)}, f32[256]{0:T(256)S(1)}, f32[256]{0:T(256)S(1)}, bf16[1024]{0:T(1024)(128)(2,1)S(1)}, f32[256,1024]{1,0:T(8,128)}) fusion(bf16[256,1024]{1,0:T(8,128)(2,1)S(1)} %copy-done.1, f32[256]{0:T(256)S(1)} %add_rsqrt_fusion, f32[256]{0:T(256)S(1)} %broadcast_multiply_fusion.2, f32[1024]{0:T(1024)S(1)} %copy-done.4, ...), kind=kOutput, calls=%fused_computation.18 | convolution fusion | flops 271185408 | bytes 2896128 | tf_op jit(solution)/shard_map/dot_general | solution.py:21
  9.3 0.1 pad_maximum_fusion
  9.4 0.7 copy.15
  10.1 24.0 %all_to_all.10 = bf16[16,72,512]{2,1,0:T(8,128)(2,1)S(1)} all-to-all(bf16[16,72,512]{2,1,0:T(8,128)(2,1)S(1)} %copy.15), channel_id=1, replica_groups=mesh['dp'=32,'bal'=16] {'bal'}, dimensions={0} | all-to-all | bytes 2359296 | tf_op jit(solution)/shard_map/all_to_all | solution.py:73
  34.0 0.2 convert_reduce_fusion
  34.2 0.6 fusion.28
  36.2 0.9 %pad_maximum_fusion.1 = bf16[32,8,512]{2,1,0:T(8,128)(2,1)} fusion(bf16[32,6,512]{2,1,0:T(8,128)(2,1)S(1)} %broadcast_in_dim.84, bf16[32,2,512]{2,1,0:T(2,128)(2,1)S(1)} %reshape.107), kind=kLoop, calls=%fused_computation.29 | loop fusion | flops 524288 | bytes 524288 | tf_op jit(solution)/shard_map/concatenate | solution.py:80
  37.1 15.3 %all-to-all-start.1 = ((bf16[32,8,512]{2,1,0:T(8,128)(2,1)}), bf16[32,8,512]{2,1,0:T(8,128)(2,1)S(1)}, u32[]{:S(2)}, u32[]{:S(2)}) async-start(bf16[32,8,512]{2,1,0:T(8,128)(2,1)} %pad_maximum_fusion.1), calls=%async_computation.1 | async-start | bytes 524288 | tf_op jit(solution)/shard_map/all_to_all | solution.py:83
  52.4 1.2 %fusion.10 = bf16[256,1024]{1,0:T(8,128)(2,1)} fusion(bf16[256,1024]{1,0:T(8,128)(2,1)S(1)} %copy-done.1, f32[256,1024]{1,0:T(8,128)S(1)} %copy-done.2, f32[256]{0:T(256)S(1)} %get-tuple-element.17, f32[256]{0:T(256)S(1)} %get-tuple-element.18, f32[1024]{0:T(1024)S(1)} %copy-done.4, f32[256]{0:T(256)S(1)} %add_rsqrt_fusion, ...), kind=kLoop, calls=%fused_computation.15 | loop fusion | flops 2621440 | bytes 2105600 | tf_op jit(solution)/shard_map/convert_element_type | solution.py:33
  53.6 13.3 %all-to-all-done.1 = bf16[32,8,512]{2,1,0:T(8,128)(2,1)S(1)} async-done(((bf16[32,8,512]{2,1,0:T(8,128)(2,1)}), bf16[32,8,512]{2,1,0:T(8,128)(2,1)S(1)}, u32[]{:S(2)}, u32[]{:S(2)}) %all-to-all-start.1) | async-done | bytes 262176 | tf_op jit(solution)/shard_map/all_to_all | solution.py:83
  67.0 0.6 fusion.29
  68.9 0.6 slice.59
  69.5 0.6 slice_bitcast_fusion
  70.1 0.6 copy.17
  70.7 0.6 copy.16
  (26 shorter events, 0.2 us)
Async XLA Ops:
  0.6 7.0 %copy-start = (bf16[1024,512]{1,0:T(8,128)(2,1)S(1)}, bf16[1024,512]{1,0:T(8,128)(2,1)}, u32[]{:S(2)}) copy-start(bf16[1024,512]{1,0:T(8,128)(2,1)} %param.9) | copy-start | bytes 3145732
  0.6 3.6 %copy-start.1 = (bf16[256,1024]{1,0:T(8,128)(2,1)S(1)}, bf16[256,1024]{1,0:T(8,128)(2,1)}, u32[]{:S(2)}) copy-start(bf16[256,1024]{1,0:T(8,128)(2,1)} %param.7) | copy-start | bytes 1572868
  0.7 3.4 %copy-start.3 = (bf16[256,512]{1,0:T(8,128)(2,1)S(1)}, bf16[256,512]{1,0:T(8,128)(2,1)}, u32[]{:S(2)}) copy-start(bf16[256,512]{1,0:T(8,128)(2,1)} %param.8) | copy-start | bytes 786436
  0.7 3.6 %copy-start.4 = (f32[1024]{0:T(1024)S(1)}, f32[1024]{0:T(1024)}, u32[]{:S(2)}) copy-start(f32[1024]{0:T(1024)} %param.10) | copy-start | bytes 12292
  0.7 3.6 %copy-start.5 = (f32[1024]{0:T(1024)S(1)}, f32[1024]{0:T(1024)}, u32[]{:S(2)}) copy-start(f32[1024]{0:T(1024)} %param.11) | copy-start | bytes 12292
  34.2 18.2 %copy-start.2 = (f32[256,1024]{1,0:T(8,128)S(1)}, f32[256,1024]{1,0:T(8,128)}, u32[]{:S(2)}) copy-start(f32[256,1024]{1,0:T(8,128)} %get-tuple-element.16) | copy-start | bytes 3145732
  37.1 29.8 %all-to-all-start.1 = ((bf16[32,8,512]{2,1,0:T(8,128)(2,1)}), bf16[32,8,512]{2,1,0:T(8,128)(2,1)S(1)}, u32[]{:S(2)}, u32[]{:S(2)}) async-start(bf16[32,8,512]{2,1,0:T(8,128)(2,1)} %pad_maximum_fusion.1), calls=%async_computation.1 | async-start | bytes 524288 | tf_op jit(solution)/shard_map/all_to_all | solution.py:83

commit v2 on v1

v2 whole, which is shorter than its diff:
```python
import functools

import jax
import jax.numpy as jnp
from jax import lax
from jax.experimental import pallas as pl
from jax.experimental.pallas import tpu as pltpu
from jax.sharding import PartitionSpec as P

epsilon = 1e-06
LANES = 128
SUBLANES = 8
COUNT_BASE = 256


def normalise(x_rows):
    x_float = x_rows.astype(jnp.float32)
    centred = x_float - jnp.mean(x_float, axis=1, keepdims=True)
    inv_std = lax.rsqrt(jnp.mean(centred * centred, axis=1, keepdims=True) + epsilon)
    return centred * inv_std, inv_std


def live_cotangent(count_ref, cot_ref):
    row = lax.broadcasted_iota(jnp.int32, cot_ref.shape, 0)
    cot = cot_ref[...]
    return jnp.where(row < count_ref[0], cot, jnp.zeros_like(cot))


def backproject(cot_live, weight_ref):
    return lax.dot_general(
        cot_live,
        weight_ref[...],
        (((1,), (1,)), ((), ())),
        preferred_element_type=jnp.float32,
    )


def count_row(count, width):
    high = jnp.floor(count * (1.0 / COUNT_BASE))
    low = count - high * COUNT_BASE
    lane = lax.broadcasted_iota(jnp.int32, (1, width), 1)
    return jnp.where(lane == 0, high, jnp.where(lane == 1, low, 0.0))


def count_of(row):
    lane = lax.broadcasted_iota(jnp.int32, row.shape, 1)
    place = jnp.where(lane == 0, float(COUNT_BASE), jnp.where(lane == 1, 1.0, 0.0))
    return jnp.sum(row * place, axis=1, keepdims=True)


def sums_kernel(
    dp,
    bal,
    count_ref,
    x_hbm,
    cot_hbm,
    weight_hbm,
    gain_hbm,
    beta_hbm,
    out_ref,
    x_ref,
    cot_ref,
    weight_ref,
    gain_ref,
    beta_ref,
    grad_w,
    small,
    arrived,
):
    copies = [
        pltpu.make_async_copy(source, target, arrived.at[index])
        for index, (source, target) in enumerate(
            (
                (x_hbm, x_ref),
                (gain_hbm, gain_ref),
                (beta_hbm, beta_ref),
                (cot_hbm, cot_ref),
                (weight_hbm, weight_ref),
            )
        )
    ]
    for copy in copies:
        copy.start()
    width, decoder = weight_ref.shape
    own = width // (dp * bal)
    vectors = width // decoder
    copies[0].wait()
    normed, _ = normalise(x_ref[...])
    for copy in copies[1:4]:
        copy.wait()
    hidden = (normed * gain_ref[...] + beta_ref[...]).astype(jnp.bfloat16)
    cot_live = live_cotangent(count_ref, cot_ref)
    product = lax.dot_general(
        hidden, cot_live, (((0,), (0,)), ((), ())), preferred_element_type=jnp.float32
    )
    for tile in range(decoder // LANES):
        grad_w[tile] = product[:, tile * LANES : (tile + 1) * LANES]
    copies[4].wait()
    grad_h = backproject(cot_live, weight_ref)
    grad_gain = jnp.sum(grad_h * normed, axis=0, keepdims=True)
    grad_beta = jnp.sum(grad_h, axis=0, keepdims=True)
    small[...] = jnp.zeros_like(small)
    for part in range(vectors):
        at = slice(part * decoder, (part + 1) * decoder)
        small[part : part + 1] = grad_gain[:, at]
        small[vectors + part : vectors + part + 1] = grad_beta[:, at]
    at = 2 * vectors
    small[at : at + 1] = jnp.sum(cot_live.astype(jnp.float32), axis=0, keepdims=True)
    small[at + 1 : at + 2] = count_row(
        jnp.full((1, 1), count_ref[0], jnp.int32).astype(jnp.float32), decoder
    )
    small_sent = small[...].astype(jnp.bfloat16)
    for owner in range(bal):
        for row in range(own):
            rows = pl.ds(owner * own + row, dp, stride=bal * own)
            for tile in range(decoder // LANES):
                out_ref[owner, row * dp : (row + 1) * dp, tile * LANES : (tile + 1) * LANES] = (
                    grad_w[tile, rows, :].astype(jnp.bfloat16)
                )
        out_ref[owner, own * dp :, :] = small_sent


def regroup_kernel(dp, own, got_ref, out_ref, spread):
    decoder = got_ref.shape[2]
    rows = out_ref.shape[1]
    total = jnp.sum(got_ref[...].astype(jnp.float32), axis=0)
    kept = rows - own
    small = total[own * dp :]
    count = count_row(count_of(small[kept - 1 : kept]), decoder)
    for tile in range(decoder // LANES):
        at = slice(tile * LANES, (tile + 1) * LANES)
        for row in range(own):
            spread[tile, pl.ds(row, dp, stride=rows), :] = total[row * dp : (row + 1) * dp, at]
        for row in range(kept):
            line = count[:, at] if row == kept - 1 else small[row : row + 1, at]
            spread[tile, pl.ds(own + row, dp, stride=rows), :] = jnp.broadcast_to(
                line, (dp, LANES)
            )
        out_ref[:, :, at] = spread[tile].reshape(dp, rows, LANES).astype(jnp.bfloat16)


def finish_kernel(own, vectors, got_ref, weight_ref, gain_ref, beta_ref, bias_ref):
    total = jnp.sum(got_ref[...].astype(jnp.float32), axis=0)
    decoder = total.shape[1]
    at = own + 2 * vectors
    scaled = total * lax.rsqrt(count_of(total[at + 1 : at + 2]))
    weight_ref[...] = scaled[:own]
    for part in range(vectors):
        lanes = slice(part * decoder, (part + 1) * decoder)
        gain_ref[:, lanes] = scaled[own + part : own + part + 1]
        beta_ref[:, lanes] = scaled[own + vectors + part : own + vectors + part + 1]
    bias_ref[...] = scaled[at : at + 1]


def rows_kernel(count_ref, x_ref, cot_ref, weight_ref, gain_ref, out_ref):
    normed, inv_std = normalise(x_ref[...])
    scaled = backproject(live_cotangent(count_ref, cot_ref), weight_ref) * gain_ref[...]
    out_ref[...] = (
        inv_std
        * (
            scaled
            - jnp.mean(scaled, axis=1, keepdims=True)
            - normed * jnp.mean(scaled * normed, axis=1, keepdims=True)
        )
    ).astype(jnp.bfloat16)


VMEM = pl.BlockSpec(memory_space=pltpu.VMEM)
HBM = pl.BlockSpec(memory_space=pltpu.HBM)
SMEM = pl.BlockSpec(memory_space=pltpu.SMEM)
PARAMS = pltpu.CompilerParams(vmem_limit_bytes=32 * 1024 * 1024)


def cost(flops, transfers):
    return pl.CostEstimate(flops=flops, bytes_accessed=transfers, transcendentals=0)


def make_body(dp, bal):
    def body(counts, rows, cotangent, weight, gain, beta):
        count, width = rows.shape
        decoder = cotangent.shape[1]
        own = width // (dp * bal)
        vectors = width // decoder
        tiles = decoder // LANES
        kept = 2 * vectors + 2
        sent = own * dp + SUBLANES
        gain = gain.reshape(1, width)
        beta = beta.reshape(1, width)
        whole = (rows, cotangent, weight, gain, beta)
        work = 2 * count * width * decoder
        first = pl.pallas_call(
            functools.partial(sums_kernel, dp, bal),
            out_shape=jax.ShapeDtypeStruct((bal, sent, decoder), jnp.bfloat16),
            in_specs=[SMEM] + [HBM] * 5,
            out_specs=VMEM,
            scratch_shapes=[
                pltpu.VMEM(rows.shape, rows.dtype),
                pltpu.VMEM(cotangent.shape, cotangent.dtype),
                pltpu.VMEM(weight.shape, weight.dtype),
                pltpu.VMEM((1, width), jnp.float32),
                pltpu.VMEM((1, width), jnp.float32),
                pltpu.VMEM((tiles, width, LANES), jnp.float32),
                pltpu.VMEM((SUBLANES, decoder), jnp.float32),
                pltpu.SemaphoreType.DMA((5,)),
            ],
            compiler_params=PARAMS,
            cost_estimate=cost(2 * work, 3000000),
            name="sums",
        )(counts, *(pltpu.with_memory_space_constraint(each, pltpu.HBM) for each in whole))
        first = lax.all_to_all(first, "bal", 0, 0, tiled=True)
        second = pl.pallas_call(
            functools.partial(regroup_kernel, dp, own),
            out_shape=jax.ShapeDtypeStruct((dp, own + kept, decoder), jnp.bfloat16),
            in_specs=[VMEM],
            out_specs=VMEM,
            scratch_shapes=[pltpu.VMEM((tiles, dp * (own + kept), LANES), jnp.float32)],
            compiler_params=PARAMS,
            cost_estimate=cost(1000000, 1500000),
            name="regroup",
        )(first)
        second, rows, cotangent = lax.optimization_barrier((second, rows, cotangent))
        grad_rows = pl.pallas_call(
            rows_kernel,
            out_shape=jax.ShapeDtypeStruct((count, width), jnp.bfloat16),
            in_specs=[SMEM] + [VMEM] * 4,
            out_specs=VMEM,
            compiler_params=PARAMS,
            cost_estimate=cost(work, 3000000),
            name="rows",
        )(counts, rows, cotangent, weight, gain)
        second = lax.all_to_all(second, "dp", 0, 0, tiled=True)
        vector = jax.ShapeDtypeStruct((1, width), jnp.float32)
        grad_weight, grad_gain, grad_beta, grad_bias = pl.pallas_call(
            functools.partial(finish_kernel, own, vectors),
            out_shape=(
                jax.ShapeDtypeStruct((own, decoder), jnp.float32),
                vector,
                vector,
                jax.ShapeDtypeStruct((1, decoder), jnp.float32),
            ),
            in_specs=[VMEM],
            out_specs=(VMEM,) * 4,
            compiler_params=PARAMS,
            cost_estimate=cost(1000000, 300000),
            name="finish",
        )(second)
        return (
            grad_rows,
            grad_weight,
            grad_gain.reshape(width),
            grad_beta.reshape(width),
            grad_bias.reshape(decoder),
        )

    return body


def solution(mesh):
    placed = (P(("dp", "bal")), P(("dp", "bal"), None), P(("dp", "bal"), None), P(), P(), P())
    return jax.shard_map(
        make_body(mesh.shape["dp"], mesh.shape["bal"]),
        mesh=mesh,
        in_specs=placed,
        out_specs=(P(("dp", "bal"), None), P(("dp", "bal"), None), P(), P(), P()),
        check_vma=False,
    )
```

time: 71.6 us -> 61.4 us (0.86)
  Pallas kernels: 0 us -> 7.61 us
  local copies, waits for them, and re-layouts: 7 us -> 0.01 us
  other arithmetic: 5.08 us -> 0 us
  between operations: 4.36 us -> 1.33 us
  matrix products: 2.27 us -> 0 us
    pallas_call x0 -> x4, Pallas kernels: none -> 7.61 us  [the longest x1 4.27 us: body(): pl.pallas_call(functools.partial(sums_kernel, dp, bal), out_shape=jax.Sha...]
    reduce_sum x5 -> x0, other arithmetic: 2.86 us -> none  [the longest x1 1.32 us: row_grads(): jnp.mean(centred * centred, axis=1, keepdims=True) + epsilon]
    reshape x5 -> x0, local copies, waits for them, and re-layouts: 2.74 us -> none  [the longest x2 2.69 us: body(): blocks = grad_w.reshape(dp, bal, own, decoder).transpose(1, 0, 2, 3)]
    dot_general x2 -> x0, matrix products: 2.27 us -> none  [the longest x1 1.6 us: row_grads(): lax.dot_general(cot_live, weight, (((1,), (1,)), ((), ())), preferred_ele...]
    unnamed x15 -> x8, local copies, waits for them, and re-layouts: 1.81 us -> 0.01 us
    slice x5 -> x0, local copies, waits for them, and re-layouts: 1.76 us -> none  [the longest x1 0.58 us: body(): small[at, 1].astype(jnp.int32)]
    convert_element_type x3 -> x0, other arithmetic: 1.21 us -> none  [the longest x1 1.19 us: row_grads(): jnp.where(row_mask, grad_x, jnp.zeros_like(grad_x)).astype(jnp.bfloat16)]
    concatenate x2 -> x0, other arithmetic: 0.96 us -> none  [the longest x1 0.85 us: body(): jnp.concatenate([part, jnp.broadcast_to(small[None], (dp,) + small.shape)...]
  transfers between devices with their start and end apart: 1 -> 1, of which waited for: 1 -> 1; matrix products, arithmetic and copies ran while one was open for 2% -> 0% of each run, Pallas kernels for 0% -> 3%
where the time goes in v2:
time: 61.4 us; the launch traced here: 61.1 us
  blocking collectives  24 us (39%)
  starting transfers between devices  15.3 us (25%)
  waiting for transfers between devices  12.9 us (21%)
  Pallas kernels  7.61 us (12%)
  between operations  1.33 us (2%)
    all_to_all x1, blocking collectives, body(): first = lax.all_to_all(first, 'bal', 0, 0, tiled=True)  24 us
    all_to_all x1, starting transfers between devices, body(): second = lax.all_to_all(second, 'dp', 0, 0, tiled=True)  15.3 us
    all_to_all x1, waiting for transfers between devices, body(): second = lax.all_to_all(second, 'dp', 0, 0, tiled=True)  12.9 us
    pallas_call x1, Pallas kernels, body(): pl.pallas_call(functools.partial(sums_kernel, dp, bal), out_shape=jax.Sha...  4.27 us
    pallas_call x1, Pallas kernels, body(): pl.pallas_call(rows_kernel, out_shape=jax.ShapeDtypeStruct((count, width)...  1.58 us
  transfers between devices with their start and end apart: 1, of which 1 were waited for; matrix products, arithmetic and copies ran while one was open for 0% of the time, Pallas kernels for 3%

profile of v2, /device:TPU:8, one launch (start us, length us, event | category | flops | bytes accessed | tf_op | source)
XLA Modules:
  0.0 61.1 jit_solution(7389654978464405485)
XLA Ops:
  1.3 4.3 %sums.1 = bf16[16,72,512]{2,1,0:T(8,128)(2,1)S(1)} custom-call(s32[1]{0:T(128)S(6)} %copy.11.count_ref, bf16[256,1024]{1,0:T(8,128)(2,1)} %x_ref, bf16[256,512]{1,0:T(8,128)(2,1)} %cot_ref, bf16[1024,512]{1,0:T(8,128)(2,1)} %weight_ref.1, f32[1,1024]{1,0:T(1,128)} %bitcast.5, f32[1,1024]{1,0:T(1,128)} %bitcast.7), custom_call_target="tpu_custom_call" | custom-call | flops 536870912 | bytes 3000000 | tf_op jit(solution)/shard_map/sums/pallas_call | solution.py:191
  5.6 24.0 %all_to_all.10.got_ref = bf16[16,72,512]{2,1,0:T(8,128)(2,1)S(1)} all-to-all(bf16[16,72,512]{2,1,0:T(8,128)(2,1)S(1)} %sums.1), channel_id=1, replica_groups=mesh['dp'=32,'bal'=16] {'bal'}, dimensions={0} | all-to-all | bytes 2359296 | tf_op jit(solution)/shard_map/all_to_all | solution.py:210
  29.5 0.0 copy-start
  29.5 0.0 copy-start.1
  29.5 0.0 copy-start.2
  29.5 0.0 copy-start.3
  29.5 1.0 %regroup.1 = bf16[32,8,512]{2,1,0:T(8,128)(2,1)} custom-call(bf16[16,72,512]{2,1,0:T(8,128)(2,1)S(1)} %all_to_all.10.got_ref), custom_call_target="tpu_custom_call" | custom-call | flops 1000000 | bytes 1500000 | tf_op jit(solution)/shard_map/regroup/pallas_call | solution.py:211
  30.6 15.3 %all-to-all-start.1 = ((bf16[32,8,512]{2,1,0:T(8,128)(2,1)}), bf16[32,8,512]{2,1,0:T(8,128)(2,1)S(1)}, u32[]{:S(2)}, u32[]{:S(2)}) async-start(bf16[32,8,512]{2,1,0:T(8,128)(2,1)} %regroup.1), calls=%async_computation.1 | async-start | bytes 524288 | tf_op jit(solution)/shard_map/all_to_all | solution.py:231
  45.8 0.0 copy-done
  45.8 0.0 copy-done.1
  45.9 0.0 copy-done.2
  45.9 0.0 copy-done.3
  45.9 1.6 %rows.1 = bf16[256,1024]{1,0:T(8,128)(2,1)} custom-call(s32[1]{0:T(128)S(6)} %copy.11.count_ref, bf16[256,1024]{1,0:T(8,128)(2,1)S(1)} %copy-done.1, bf16[256,512]{1,0:T(8,128)(2,1)S(1)} %copy-done.2, bf16[1024,512]{1,0:T(8,128)(2,1)S(1)} %copy-done, f32[1,1024]{1,0:T(1,128)S(1)} %bitcast.6), custom_call_target="tpu_custom_call" | custom-call | flops 268435456 | bytes 3000000 | tf_op jit(solution)/shard_map/rows/pallas_call | solution.py:222
  47.5 12.9 %all-to-all-done.1.got_ref = bf16[32,8,512]{2,1,0:T(8,128)(2,1)S(1)} async-done(((bf16[32,8,512]{2,1,0:T(8,128)(2,1)}), bf16[32,8,512]{2,1,0:T(8,128)(2,1)S(1)}, u32[]{:S(2)}, u32[]{:S(2)}) %all-to-all-start.1) | async-done | bytes 262176 | tf_op jit(solution)/shard_map/all_to_all | solution.py:231
  60.4 0.7 %finish.1 = (f32[2,512]{1,0:T(2,128)}, f32[1,1024]{1,0:T(1,128)}, f32[1,1024]{1,0:T(1,128)}, f32[1,512]{1,0:T(1,128)}) custom-call(bf16[32,8,512]{2,1,0:T(8,128)(2,1)S(1)} %all-to-all-done.1.got_ref), custom_call_target="tpu_custom_call" | custom-call | flops 1000000 | bytes 300000 | tf_op jit(solution)/shard_map/finish/pallas_call | solution.py:233
Async XLA Ops:
  29.5 16.3 %copy-start = (bf16[1024,512]{1,0:T(8,128)(2,1)S(1)}, bf16[1024,512]{1,0:T(8,128)(2,1)}, u32[]{:S(2)}) copy-start(bf16[1024,512]{1,0:T(8,128)(2,1)} %weight_ref.1) | copy-start | bytes 3145732
  29.5 16.3 %copy-start.1 = (bf16[256,1024]{1,0:T(8,128)(2,1)S(1)}, bf16[256,1024]{1,0:T(8,128)(2,1)}, u32[]{:S(2)}) copy-start(bf16[256,1024]{1,0:T(8,128)(2,1)} %x_ref) | copy-start | bytes 1572868
  29.5 16.3 %copy-start.2 = (bf16[256,512]{1,0:T(8,128)(2,1)S(1)}, bf16[256,512]{1,0:T(8,128)(2,1)}, u32[]{:S(2)}) copy-start(bf16[256,512]{1,0:T(8,128)(2,1)} %cot_ref) | copy-start | bytes 786436
  29.5 16.3 %copy-start.3 = (f32[1024]{0:T(1024)S(1)}, f32[1024]{0:T(1024)}, u32[]{:S(2)}) copy-start(f32[1024]{0:T(1024)} %param.10) | copy-start | bytes 12292
  30.6 29.8 %all-to-all-start.1 = ((bf16[32,8,512]{2,1,0:T(8,128)(2,1)}), bf16[32,8,512]{2,1,0:T(8,128)(2,1)S(1)}, u32[]{:S(2)}, u32[]{:S(2)}) async-start(bf16[32,8,512]{2,1,0:T(8,128)(2,1)} %regroup.1), calls=%async_computation.1 | async-start | bytes 524288 | tf_op jit(solution)/shard_map/all_to_all | solution.py:231

commit v3 on v2

v3 whole, which is shorter than its diff:
```python
import functools

import jax
import jax.numpy as jnp
from jax import lax
from jax.experimental import pallas as pl
from jax.experimental.pallas import tpu as pltpu
from jax.sharding import PartitionSpec as P

epsilon = 1e-06
LANES = 128
SUBLANES = 8
CORES = 2
COUNT_BASE = 256


def ring(step, size):
    return min(step % size, -step % size)


def bal_order(bal):
    return sorted(
        range(bal), key=lambda at: (-2 * ring(at // 4, bal // 4) - at // 2 % 2 - 0.5 * (at % 2), at)
    )


def dp_order(dp):
    size_y, size_z = dp // 4, 4
    start = (size_y // 2, size_z // 2)

    def distance(at):
        return ring(at // size_z - start[0], size_y) + 2 * ring(at % size_z - start[1], size_z)

    return sorted(range(dp), key=lambda at: (distance(at), at))


def normalise(x_rows):
    x_float = x_rows.astype(jnp.float32)
    centred = x_float - jnp.mean(x_float, axis=1, keepdims=True)
    inv_std = lax.rsqrt(jnp.mean(centred * centred, axis=1, keepdims=True) + epsilon)
    return centred * inv_std, inv_std


def live_cotangent(count_ref, cot_ref):
    row = lax.broadcasted_iota(jnp.int32, cot_ref.shape, 0)
    cot = cot_ref[...]
    return jnp.where(row < count_ref[0], cot, jnp.zeros_like(cot))


def backproject(cot_live, weight_ref):
    return lax.dot_general(
        cot_live,
        weight_ref[...],
        (((1,), (1,)), ((), ())),
        preferred_element_type=jnp.float32,
    )


def project(hidden, cot_live):
    return lax.dot_general(
        hidden, cot_live, (((0,), (0,)), ((), ())), preferred_element_type=jnp.float32
    )


def start_copies(arrived, *pairs):
    copies = [
        pltpu.make_async_copy(source, target, arrived.at[index])
        for index, (source, target) in enumerate(pairs)
    ]
    for copy in copies:
        copy.start()
    return copies


def count_row(count, width):
    high = jnp.floor(count * (1.0 / COUNT_BASE))
    low = count - high * COUNT_BASE
    lane = lax.broadcasted_iota(jnp.int32, (1, width), 1)
    return jnp.where(lane == 0, high, jnp.where(lane == 1, low, 0.0))


def count_of(row):
    lane = lax.broadcasted_iota(jnp.int32, row.shape, 1)
    place = jnp.where(lane == 0, float(COUNT_BASE), jnp.where(lane == 1, 1.0, 0.0))
    return jnp.sum(row * place, axis=1, keepdims=True)


def prepare_kernel(
    count_ref,
    x_hbm,
    cot_hbm,
    gain_hbm,
    beta_hbm,
    send_ref,
    hidden_ref,
    normed_ref,
    live_ref,
    x_ref,
    cot_ref,
    gain_ref,
    beta_ref,
    arrived,
):
    copies = start_copies(
        arrived,
        (x_hbm, x_ref),
        (gain_hbm, gain_ref),
        (beta_hbm, beta_ref),
        (cot_hbm, cot_ref),
    )
    half = hidden_ref.shape[2]
    copies[0].wait()
    normed, _ = normalise(x_ref[...])
    normed_ref[...] = normed
    for copy in copies[1:]:
        copy.wait()
    hidden = (normed * gain_ref[...] + beta_ref[...]).astype(jnp.bfloat16)
    for part in range(CORES):
        hidden_ref[part] = hidden[:, part * half : (part + 1) * half]
    cot_live = live_cotangent(count_ref, cot_ref)
    live_ref[...] = cot_live
    send_ref[:, half:] = cot_live
    send_ref[:, :half] = hidden_ref[1 - lax.axis_index("bal") % CORES]


def own_kernel(
    count_ref, hidden_ref, normed_ref, live_ref, weight_hbm, product_ref, small, weight_ref, arrived
):
    copies = start_copies(arrived, (weight_hbm, weight_ref))
    width, decoder = weight_ref.shape
    vectors = width // decoder
    cot_live = live_ref[...]
    product_ref[...] = project(hidden_ref[lax.axis_index("bal") % CORES], cot_live)
    copies[0].wait()
    grad_h = backproject(cot_live, weight_ref)
    grad_gain = jnp.sum(grad_h * normed_ref[...], axis=0, keepdims=True)
    grad_beta = jnp.sum(grad_h, axis=0, keepdims=True)
    small[...] = jnp.zeros_like(small)
    for part in range(vectors):
        at = slice(part * decoder, (part + 1) * decoder)
        small[part : part + 1] = grad_gain[:, at]
        small[vectors + part : vectors + part + 1] = grad_beta[:, at]
    at = 2 * vectors
    small[at : at + 1] = jnp.sum(cot_live.astype(jnp.float32), axis=0, keepdims=True)
    small[at + 1 : at + 2] = count_row(
        jnp.full((1, 1), count_ref[0], jnp.int32).astype(jnp.float32), decoder
    )


def pair_kernel(dp, bal, own, got_ref, product_ref, small_ref, out_ref, grad_w):
    span = bal * own
    pitch = span + 1
    peers = dp // CORES
    half, decoder = product_ref.shape
    product = product_ref[...] + project(got_ref[:, :half], got_ref[:, half:])
    for tile in range(decoder // LANES):
        at = slice(tile * LANES, (tile + 1) * LANES)
        for peer in range(peers):
            grad_w[tile, peer * pitch : peer * pitch + span] = product[
                peer * span : (peer + 1) * span, at
            ]
    small = small_ref[...].astype(jnp.bfloat16)
    for place, owner in enumerate(bal_order(bal)):
        for tile in range(decoder // LANES):
            at = slice(tile * LANES, (tile + 1) * LANES)
            for row in range(own):
                rows = pl.ds(owner * own + row, peers, stride=pitch)
                out_ref[place, row * peers : (row + 1) * peers, at] = grad_w[
                    tile, rows, :
                ].astype(jnp.bfloat16)
        out_ref[place, own * peers :, :] = small


def regroup_kernel(dp, own, got_ref, out_ref, spread):
    bal, _, decoder = got_ref.shape
    rows = out_ref.shape[1]
    kept = rows - own
    peers = dp // CORES
    halves = [0.0] * CORES
    for place, member in enumerate(bal_order(bal)):
        halves[member % CORES] += got_ref[place].astype(jnp.float32)
    small = sum(part[own * peers :] for part in halves)
    count = count_row(count_of(small[kept - 1 : kept]), decoder)
    for tile in range(decoder // LANES):
        at = slice(tile * LANES, (tile + 1) * LANES)
        for core in range(CORES):
            for row in range(own):
                spread[tile, pl.ds(core * peers * rows + row, peers, stride=rows), :] = halves[
                    core
                ][row * peers : (row + 1) * peers, at]
        for row in range(kept):
            line = count[:, at] if row == kept - 1 else small[row : row + 1, at]
            spread[tile, pl.ds(own + row, dp, stride=rows), :] = jnp.broadcast_to(
                line, (dp, LANES)
            )
        for place, peer in enumerate(dp_order(dp)):
            out_ref[place, :, at] = spread[tile, peer * rows : (peer + 1) * rows].astype(
                jnp.bfloat16
            )


def finish_kernel(own, vectors, got_ref, weight_ref, gain_ref, beta_ref, bias_ref):
    total = jnp.sum(got_ref[...].astype(jnp.float32), axis=0)
    decoder = total.shape[1]
    at = own + 2 * vectors
    scaled = total * lax.rsqrt(count_of(total[at + 1 : at + 2]))
    weight_ref[...] = scaled[:own]
    for part in range(vectors):
        lanes = slice(part * decoder, (part + 1) * decoder)
        gain_ref[:, lanes] = scaled[own + part : own + part + 1]
        beta_ref[:, lanes] = scaled[own + vectors + part : own + vectors + part + 1]
    bias_ref[...] = scaled[at : at + 1]


def rows_kernel(
    count_ref,
    x_hbm,
    cot_hbm,
    weight_hbm,
    gain_hbm,
    out_ref,
    x_ref,
    cot_ref,
    weight_ref,
    gain_ref,
    arrived,
):
    copies = start_copies(
        arrived,
        (x_hbm, x_ref),
        (gain_hbm, gain_ref),
        (cot_hbm, cot_ref),
        (weight_hbm, weight_ref),
    )
    copies[0].wait()
    normed, inv_std = normalise(x_ref[...])
    for copy in copies[1:]:
        copy.wait()
    scaled = backproject(live_cotangent(count_ref, cot_ref), weight_ref) * gain_ref[...]
    out_ref[...] = (
        inv_std
        * (
            scaled
            - jnp.mean(scaled, axis=1, keepdims=True)
            - normed * jnp.mean(scaled * normed, axis=1, keepdims=True)
        )
    ).astype(jnp.bfloat16)


VMEM = pl.BlockSpec(memory_space=pltpu.VMEM)
SMEM = pl.BlockSpec(memory_space=pltpu.SMEM)
HBM = pl.BlockSpec(memory_space=pltpu.HBM)
PARAMS = pltpu.CompilerParams(vmem_limit_bytes=32 * 1024 * 1024)


def cost(flops, transfers):
    return pl.CostEstimate(flops=flops, bytes_accessed=transfers, transcendentals=0)


def in_hbm(*arrays):
    return tuple(pltpu.with_memory_space_constraint(each, pltpu.HBM) for each in arrays)


def scratch_of(*arrays):
    return [pltpu.VMEM(each.shape, each.dtype) for each in arrays] + [
        pltpu.SemaphoreType.DMA((len(arrays),))
    ]


def exchange(blocks, axis, order):
    return lax.all_to_all(blocks, axis, 0, 0, tiled=True, axis_index_groups=[order])


def make_body(dp, bal):
    def body(counts, rows, cotangent, weight, gain, beta):
        count, width = rows.shape
        decoder = cotangent.shape[1]
        half = width // CORES
        own = width // (dp * bal)
        vectors = width // decoder
        tiles = decoder // LANES
        kept = 2 * vectors + 2
        peers = dp // CORES
        gain = gain.reshape(1, width)
        beta = beta.reshape(1, width)
        work = 2 * count * width * decoder
        shape = jax.ShapeDtypeStruct
        send, hidden, normed, live = pl.pallas_call(
            prepare_kernel,
            out_shape=(
                shape((count, half + decoder), jnp.bfloat16),
                shape((CORES, count, half), jnp.bfloat16),
                shape((count, width), jnp.float32),
                shape((count, decoder), jnp.bfloat16),
            ),
            in_specs=[SMEM] + [HBM] * 4,
            out_specs=(VMEM,) * 4,
            scratch_shapes=scratch_of(rows, cotangent, gain, beta),
            compiler_params=PARAMS,
            cost_estimate=cost(20 * count * width, 3000000),
            name="prepare",
        )(counts, *in_hbm(rows, cotangent, gain, beta))
        got = lax.ppermute(send, "bal", [(member, member ^ 1) for member in range(bal)])
        product, small = pl.pallas_call(
            own_kernel,
            out_shape=(
                shape((half, decoder), jnp.float32),
                shape((SUBLANES, decoder), jnp.float32),
            ),
            in_specs=[SMEM] + [VMEM] * 3 + [HBM],
            out_specs=(VMEM,) * 2,
            scratch_shapes=scratch_of(weight),
            compiler_params=PARAMS,
            cost_estimate=cost(3 * work // 2, 3000000),
            name="own",
        )(counts, hidden, normed, live, *in_hbm(weight))
        first = pl.pallas_call(
            functools.partial(pair_kernel, dp, bal, own),
            out_shape=shape((bal, own * peers + SUBLANES, decoder), jnp.bfloat16),
            in_specs=[VMEM] * 3,
            out_specs=VMEM,
            scratch_shapes=[pltpu.VMEM((tiles, peers * (bal * own + 1), LANES), jnp.float32)],
            compiler_params=PARAMS,
            cost_estimate=cost(work // 2, 2000000),
            name="pair",
        )(got, product, small)
        first = exchange(first, "bal", bal_order(bal))
        second = pl.pallas_call(
            functools.partial(regroup_kernel, dp, own),
            out_shape=shape((dp, own + kept, decoder), jnp.bfloat16),
            in_specs=[VMEM],
            out_specs=VMEM,
            scratch_shapes=[pltpu.VMEM((tiles, dp * (own + kept), LANES), jnp.float32)],
            compiler_params=PARAMS,
            cost_estimate=cost(1000000, 1500000),
            name="regroup",
        )(first)
        second, rows, cotangent = lax.optimization_barrier((second, rows, cotangent))
        grad_rows = pl.pallas_call(
            rows_kernel,
            out_shape=shape((count, width), jnp.bfloat16),
            in_specs=[SMEM] + [HBM] * 4,
            out_specs=VMEM,
            scratch_shapes=scratch_of(rows, cotangent, weight, gain),
            compiler_params=PARAMS,
            cost_estimate=cost(work, 3000000),
            name="rows",
        )(counts, *in_hbm(rows, cotangent, weight, gain))
        second = exchange(second, "dp", dp_order(dp))
        vector = shape((1, width), jnp.float32)
        grad_weight, grad_gain, grad_beta, grad_bias = pl.pallas_call(
            functools.partial(finish_kernel, own, vectors),
            out_shape=(
                shape((own, decoder), jnp.float32),
                vector,
                vector,
                shape((1, decoder), jnp.float32),
            ),
            in_specs=[VMEM],
            out_specs=(VMEM,) * 4,
            compiler_params=PARAMS,
            cost_estimate=cost(1000000, 300000),
            name="finish",
        )(second)
        return (
            grad_rows,
            grad_weight,
            grad_gain.reshape(width),
            grad_beta.reshape(width),
            grad_bias.reshape(decoder),
        )

    return body


def solution(mesh):
    placed = (P(("dp", "bal")), P(("dp", "bal"), None), P(("dp", "bal"), None), P(), P(), P())
    return jax.shard_map(
        make_body(mesh.shape["dp"], mesh.shape["bal"]),
        mesh=mesh,
        in_specs=placed,
        out_specs=(P(("dp", "bal"), None), P(("dp", "bal"), None), P(), P(), P()),
        check_vma=False,
    )
```

time: 61.4 us -> 49.9 us (0.81)
  the two profiles are of different devices: /device:TPU:8 before, /device:TPU:1 now
where the time goes in v3:
time: 49.9 us; the launch traced here: 49.5 us
  starting transfers between devices  22.6 us (45%)
  blocking collectives  13.8 us (28%)
  Pallas kernels  8.49 us (17%)
  waiting for transfers between devices  3.35 us (7%)
  between operations  1.33 us (3%)
    all_to_all x1, starting transfers between devices, exchange(): lax.all_to_all(blocks, axis, 0, 0, tiled=True, axis_index_groups=[order])  13.8 us
    all_to_all x1, blocking collectives, exchange(): lax.all_to_all(blocks, axis, 0, 0, tiled=True, axis_index_groups=[order])  13.8 us
    ppermute x1, starting transfers between devices, body(): lax.ppermute(send, 'bal', [(member, member ^ 1) for member in range(bal)])  8.79 us
    all_to_all x1, waiting for transfers between devices, exchange(): lax.all_to_all(blocks, axis, 0, 0, tiled=True, axis_index_groups=[order])  3.34 us
    pallas_call x1, Pallas kernels, body(): pl.pallas_call(rows_kernel, out_shape=shape((count, width), jnp.bfloat16)...  2.97 us
    pallas_call x1, Pallas kernels, body(): pl.pallas_call(prepare_kernel, out_shape=(shape((count, half + decoder),...  1.74 us
    pallas_call x1, Pallas kernels, body(): pl.pallas_call(own_kernel, out_shape=(shape((half, decoder), jnp.float32)...  1.73 us
  transfers between devices with their start and end apart: 2, of which 1 were waited for; matrix products, arithmetic and copies ran while one was open for 0% of the time, Pallas kernels for 10%

profile of v3, /device:TPU:1, one launch (start us, length us, event | category | flops | bytes accessed | tf_op | source)
XLA Modules:
  0.0 49.5 jit_solution(4487846690590007201)
XLA Ops:
  1.3 1.7 %prepare.1 = (bf16[256,1024]{1,0:T(8,128)(2,1)S(1)}, bf16[2,256,512]{2,1,0:T(8,128)(2,1)S(1)}, f32[256,1024]{1,0:T(8,128)S(1)}, bf16[256,512]{1,0:T(8,128)(2,1)S(1)}) custom-call(s32[1]{0:T(128)S(6)} %copy.11.count_ref, bf16[256,1024]{1,0:T(8,128)(2,1)} %x_hbm.2, bf16[256,512]{1,0:T(8,128)(2,1)} %cot_hbm.2, f32[1,1024]{1,0:T(1,128)} %bitcast.5, ...), custom_call_target="tpu_custom_call" | custom-call | flops 5242880 | bytes 3000000 | tf_op jit(solution)/shard_map/prepare/pallas_call | solution.py:288
  3.0 8.8 %collective-permute-start = (bf16[256,1024]{1,0:T(8,128)(2,1)S(1)}, bf16[256,1024]{1,0:T(8,128)(2,1)S(1)}, u32[]{:S(2)}, u32[]{:S(2)}) collective-permute-start(bf16[256,1024]{1,0:T(8,128)(2,1)S(1)} %get-tuple-element.18), channel_id=1, source_target_pairs={{0,1},{1,0},{2,3},{3,2},{4,5},{5,4},{6,7},{7,6},{8,9},{9,8},{10,11... | collective-permute-start | bytes 1572872 | tf_op jit(solution)/shard_map/ppermute | solution.py:303
  11.8 1.7 %own.1 = (f32[512,512]{1,0:T(8,128)S(1)}, f32[8,512]{1,0:T(8,128)S(1)}) custom-call(s32[1]{0:T(128)S(6)} %copy.11.count_ref, bf16[2,256,512]{2,1,0:T(8,128)(2,1)S(1)} %get-tuple-element.19.hidden_ref, f32[256,1024]{1,0:T(8,128)S(1)} %get-tuple-element.20.normed_ref, bf16[256,512]{1,0:T(8,128)(2,1)S(1)} %get-tuple-element.21.live_ref, ...), custom_call_target="tpu_custom_call" | custom-call | flops 402653184 | bytes 3000000 | tf_op jit(solution)/shard_map/own/pallas_call | solution.py:304
  13.6 0.0 collective-permute-done.got_ref
  13.6 0.4 pair.1
  14.0 13.8 %all_to_all.10.got_ref = bf16[16,40,512]{2,1,0:T(8,128)(2,1)S(1)} all-to-all(bf16[16,40,512]{2,1,0:T(8,128)(2,1)S(1)} %pair.1), channel_id=1, replica_groups={{11,10,9,8,7,15,6,14,5,13,4,12,3,2,1,0},{27,26,25,24,23,31,22,30,21,29,..., dimensions={0} | all-to-all | bytes 1310720 | tf_op jit(solution)/shard_map/all_to_all | solution.py:271
  27.8 0.9 %regroup.1 = bf16[32,8,512]{2,1,0:T(8,128)(2,1)} custom-call(bf16[16,40,512]{2,1,0:T(8,128)(2,1)S(1)} %all_to_all.10.got_ref), custom_call_target="tpu_custom_call" | custom-call | flops 1000000 | bytes 1500000 | tf_op jit(solution)/shard_map/regroup/pallas_call | solution.py:328
  28.7 13.8 %all-to-all-start.1 = ((bf16[32,8,512]{2,1,0:T(8,128)(2,1)}), bf16[32,8,512]{2,1,0:T(8,128)(2,1)S(1)}, u32[]{:S(2)}, u32[]{:S(2)}) async-start(bf16[32,8,512]{2,1,0:T(8,128)(2,1)} %regroup.1), calls=%async_computation.1 | async-start | bytes 524288 | tf_op jit(solution)/shard_map/all_to_all | solution.py:271
  42.5 3.0 %rows.1 = bf16[256,1024]{1,0:T(8,128)(2,1)} custom-call(s32[1]{0:T(128)S(6)} %copy.11.count_ref, bf16[256,1024]{1,0:T(8,128)(2,1)} %x_hbm.2, bf16[256,512]{1,0:T(8,128)(2,1)} %cot_hbm.2, bf16[1024,512]{1,0:T(8,128)(2,1)} %weight_hbm.3, f32[1,1024]{1,0:T(1,128)} %bitcast.6), custom_call_target="tpu_custom_call" | custom-call | flops 268435456 | bytes 3000000 | tf_op jit(solution)/shard_map/rows/pallas_call | solution.py:339
  45.5 3.3 %all-to-all-done.1.got_ref = bf16[32,8,512]{2,1,0:T(8,128)(2,1)S(1)} async-done(((bf16[32,8,512]{2,1,0:T(8,128)(2,1)}), bf16[32,8,512]{2,1,0:T(8,128)(2,1)S(1)}, u32[]{:S(2)}, u32[]{:S(2)}) %all-to-all-start.1) | async-done | bytes 262176 | tf_op jit(solution)/shard_map/all_to_all | solution.py:271
  48.8 0.7 %finish.1 = (f32[2,512]{1,0:T(2,128)}, f32[1,1024]{1,0:T(1,128)}, f32[1,1024]{1,0:T(1,128)}, f32[1,512]{1,0:T(1,128)}) custom-call(bf16[32,8,512]{2,1,0:T(8,128)(2,1)S(1)} %all-to-all-done.1.got_ref), custom_call_target="tpu_custom_call" | custom-call | flops 1000000 | bytes 300000 | tf_op jit(solution)/shard_map/finish/pallas_call | solution.py:351
Async XLA Ops:
  3.0 10.5 %collective-permute-start = (bf16[256,1024]{1,0:T(8,128)(2,1)S(1)}, bf16[256,1024]{1,0:T(8,128)(2,1)S(1)}, u32[]{:S(2)}, u32[]{:S(2)}) collective-permute-start(bf16[256,1024]{1,0:T(8,128)(2,1)S(1)} %get-tuple-element.18), channel_id=1, source_target_pairs={{0,1},{1,0},{2,3},{3,2},{4,5},{5,4},{6,7},{7,6},{8,9},{9,8},{10,11... | collective-permute-start | bytes 1572872 | tf_op jit(solution)/shard_map/ppermute | solution.py:303
  28.7 20.1 %all-to-all-start.1 = ((bf16[32,8,512]{2,1,0:T(8,128)(2,1)}), bf16[32,8,512]{2,1,0:T(8,128)(2,1)S(1)}, u32[]{:S(2)}, u32[]{:S(2)}) async-start(bf16[32,8,512]{2,1,0:T(8,128)(2,1)} %regroup.1), calls=%async_computation.1 | async-start | bytes 524288 | tf_op jit(solution)/shard_map/all_to_all | solution.py:271

commit v4 on v3

--- a/solution.py
+++ b/solution.py
@@ -72,10 +72,10 @@
     return copies
 
 
-def count_row(count, width):
+def count_row(count):
     high = jnp.floor(count * (1.0 / COUNT_BASE))
     low = count - high * COUNT_BASE
-    lane = lax.broadcasted_iota(jnp.int32, (1, width), 1)
+    lane = lax.broadcasted_iota(jnp.int32, (1, LANES), 1)
     return jnp.where(lane == 0, high, jnp.where(lane == 1, low, 0.0))
 
 
@@ -83,6 +83,11 @@
     lane = lax.broadcasted_iota(jnp.int32, row.shape, 1)
     place = jnp.where(lane == 0, float(COUNT_BASE), jnp.where(lane == 1, 1.0, 0.0))
     return jnp.sum(row * place, axis=1, keepdims=True)
+
+
+def put_lines(ref, start, vector):
+    for line in range(vector.shape[1] // LANES):
+        ref[start + line : start + line + 1] = vector[:, line * LANES : (line + 1) * LANES]
 
 
 def prepare_kernel(
@@ -128,22 +133,18 @@
 ):
     copies = start_copies(arrived, (weight_hbm, weight_ref))
     width, decoder = weight_ref.shape
-    vectors = width // decoder
     cot_live = live_ref[...]
     product_ref[...] = project(hidden_ref[lax.axis_index("bal") % CORES], cot_live)
     copies[0].wait()
     grad_h = backproject(cot_live, weight_ref)
     grad_gain = jnp.sum(grad_h * normed_ref[...], axis=0, keepdims=True)
-    grad_beta = jnp.sum(grad_h, axis=0, keepdims=True)
+    grad_bias = jnp.sum(cot_live.astype(jnp.float32), axis=0, keepdims=True)
     small[...] = jnp.zeros_like(small)
-    for part in range(vectors):
-        at = slice(part * decoder, (part + 1) * decoder)
-        small[part : part + 1] = grad_gain[:, at]
-        small[vectors + part : vectors + part + 1] = grad_beta[:, at]
-    at = 2 * vectors
-    small[at : at + 1] = jnp.sum(cot_live.astype(jnp.float32), axis=0, keepdims=True)
-    small[at + 1 : at + 2] = count_row(
-        jnp.full((1, 1), count_ref[0], jnp.int32).astype(jnp.float32), decoder
+    put_lines(small, 0, grad_gain)
+    put_lines(small, width // LANES, grad_bias)
+    at = (width + decoder) // LANES
+    small[at : at + 1] = count_row(
+        jnp.full((1, 1), count_ref[0], jnp.int32).astype(jnp.float32)
     )
 
 
@@ -160,56 +161,64 @@
                 peer * span : (peer + 1) * span, at
             ]
     small = small_ref[...].astype(jnp.bfloat16)
+    tiles = decoder // LANES
     for place, owner in enumerate(bal_order(bal)):
-        for tile in range(decoder // LANES):
-            at = slice(tile * LANES, (tile + 1) * LANES)
+        for tile in range(tiles):
             for row in range(own):
                 rows = pl.ds(owner * own + row, peers, stride=pitch)
-                out_ref[place, row * peers : (row + 1) * peers, at] = grad_w[
-                    tile, rows, :
-                ].astype(jnp.bfloat16)
-        out_ref[place, own * peers :, :] = small
-
-
-def regroup_kernel(dp, own, got_ref, out_ref, spread):
-    bal, _, decoder = got_ref.shape
-    rows = out_ref.shape[1]
-    kept = rows - own
+                at = (tile * own + row) * peers
+                out_ref[place, at : at + peers, :] = grad_w[tile, rows, :].astype(jnp.bfloat16)
+        out_ref[place, tiles * own * peers :, :] = small
+
+
+def regroup_kernel(dp, lines, at_count, got_ref, out_ref, spread):
+    bal = got_ref.shape[0]
     peers = dp // CORES
     halves = [0.0] * CORES
     for place, member in enumerate(bal_order(bal)):
         halves[member % CORES] += got_ref[place].astype(jnp.float32)
-    small = sum(part[own * peers :] for part in halves)
-    count = count_row(count_of(small[kept - 1 : kept]), decoder)
-    for tile in range(decoder // LANES):
-        at = slice(tile * LANES, (tile + 1) * LANES)
-        for core in range(CORES):
-            for row in range(own):
-                spread[tile, pl.ds(core * peers * rows + row, peers, stride=rows), :] = halves[
-                    core
-                ][row * peers : (row + 1) * peers, at]
-        for row in range(kept):
-            line = count[:, at] if row == kept - 1 else small[row : row + 1, at]
-            spread[tile, pl.ds(own + row, dp, stride=rows), :] = jnp.broadcast_to(
-                line, (dp, LANES)
-            )
-        for place, peer in enumerate(dp_order(dp)):
-            out_ref[place, :, at] = spread[tile, peer * rows : (peer + 1) * rows].astype(
-                jnp.bfloat16
-            )
-
-
-def finish_kernel(own, vectors, got_ref, weight_ref, gain_ref, beta_ref, bias_ref):
+    small = sum(part[lines * peers :] for part in halves)
+    line = lax.broadcasted_iota(jnp.int32, small.shape, 0)
+    count = count_of(small[at_count : at_count + 1])
+    small = jnp.where(line == at_count, count_row(count), small).astype(jnp.bfloat16)
+    for core in range(CORES):
+        for row in range(lines):
+            spread[pl.ds(core * peers * lines + row, peers, stride=lines), :] = halves[core][
+                row * peers : (row + 1) * peers
+            ]
+    for place, peer in enumerate(dp_order(dp)):
+        out_ref[place, :lines, :] = spread[peer * lines : (peer + 1) * lines].astype(jnp.bfloat16)
+        out_ref[place, lines:, :] = small
+
+
+def finish_kernel(got_ref, projection_ref, weight_ref, gain_ref, beta_ref, bias_ref):
+    width, decoder = projection_ref.shape
+    own, tiles = weight_ref.shape[0], decoder // LANES
     total = jnp.sum(got_ref[...].astype(jnp.float32), axis=0)
-    decoder = total.shape[1]
-    at = own + 2 * vectors
-    scaled = total * lax.rsqrt(count_of(total[at + 1 : at + 2]))
-    weight_ref[...] = scaled[:own]
-    for part in range(vectors):
-        lanes = slice(part * decoder, (part + 1) * decoder)
-        gain_ref[:, lanes] = scaled[own + part : own + part + 1]
-        beta_ref[:, lanes] = scaled[own + vectors + part : own + vectors + part + 1]
-    bias_ref[...] = scaled[at : at + 1]
+    at_gain = own * tiles
+    at_bias = at_gain + width // LANES
+    at_count = at_bias + tiles
+    scaled = total * lax.rsqrt(count_of(total[at_count : at_count + 1]))
+
+    def joined(start, lines):
+        return jnp.concatenate(
+            [scaled[start + line : start + line + 1] for line in range(lines)], axis=1
+        )
+
+    for tile in range(tiles):
+        weight_ref[:, tile * LANES : (tile + 1) * LANES] = scaled[tile * own : (tile + 1) * own]
+    gain_ref[...] = joined(at_gain, width // LANES)
+    bias = joined(at_bias, tiles)
+    bias_ref[...] = bias
+    row = lax.broadcasted_iota(jnp.int32, (SUBLANES, decoder), 0)
+    terms = jnp.zeros((SUBLANES, decoder), jnp.float32)
+    for term in range(3):
+        part = bias.astype(jnp.bfloat16).astype(jnp.float32)
+        terms = jnp.where(row == term, part, terms)
+        bias = bias - part
+    beta_ref[...] = jnp.sum(
+        backproject(terms.astype(jnp.bfloat16), projection_ref), axis=0, keepdims=True
+    )
 
 
 def rows_kernel(
@@ -277,9 +286,10 @@
         decoder = cotangent.shape[1]
         half = width // CORES
         own = width // (dp * bal)
-        vectors = width // decoder
         tiles = decoder // LANES
-        kept = 2 * vectors + 2
+        lines = tiles * own
+        at_count = (width + decoder) // LANES
+        kept = -(-(at_count + 1) // SUBLANES) * SUBLANES
         peers = dp // CORES
         gain = gain.reshape(1, width)
         beta = beta.reshape(1, width)
@@ -305,7 +315,7 @@
             own_kernel,
             out_shape=(
                 shape((half, decoder), jnp.float32),
-                shape((SUBLANES, decoder), jnp.float32),
+                shape((kept, LANES), jnp.float32),
             ),
             in_specs=[SMEM] + [VMEM] * 3 + [HBM],
             out_specs=(VMEM,) * 2,
@@ -316,7 +326,7 @@
         )(counts, hidden, normed, live, *in_hbm(weight))
         first = pl.pallas_call(
             functools.partial(pair_kernel, dp, bal, own),
-            out_shape=shape((bal, own * peers + SUBLANES, decoder), jnp.bfloat16),
+            out_shape=shape((bal, lines * peers + kept, LANES), jnp.bfloat16),
             in_specs=[VMEM] * 3,
             out_specs=VMEM,
             scratch_shapes=[pltpu.VMEM((tiles, peers * (bal * own + 1), LANES), jnp.float32)],
@@ -326,11 +336,11 @@
         )(got, product, small)
         first = exchange(first, "bal", bal_order(bal))
         second = pl.pallas_call(
-            functools.partial(regroup_kernel, dp, own),
-            out_shape=shape((dp, own + kept, decoder), jnp.bfloat16),
+            functools.partial(regroup_kernel, dp, lines, at_count),
+            out_shape=shape((dp, lines + kept, LANES), jnp.bfloat16),
             in_specs=[VMEM],
             out_specs=VMEM,
-            scratch_shapes=[pltpu.VMEM((tiles, dp * (own + kept), LANES), jnp.float32)],
+            scratch_shapes=[pltpu.VMEM((dp * lines, LANES), jnp.float32)],
             compiler_params=PARAMS,
             cost_estimate=cost(1000000, 1500000),
             name="regroup",
@@ -349,19 +359,19 @@
         second = exchange(second, "dp", dp_order(dp))
         vector = shape((1, width), jnp.float32)
         grad_weight, grad_gain, grad_beta, grad_bias = pl.pallas_call(
-            functools.partial(finish_kernel, own, vectors),
+            finish_kernel,
             out_shape=(
                 shape((own, decoder), jnp.float32),
                 vector,
                 vector,
                 shape((1, decoder), jnp.float32),
             ),
-            in_specs=[VMEM],
+            in_specs=[VMEM] * 2,
             out_specs=(VMEM,) * 4,
             compiler_params=PARAMS,
             cost_estimate=cost(1000000, 300000),
             name="finish",
-        )(second)
+        )(second, weight)
         return (
             grad_rows,
             grad_weight,

time: 49.9 us -> 48.2 us (0.966)
  waiting for transfers between devices: 3.35 us -> 2.09 us
  blocking collectives: 13.8 us -> 13.1 us
    all_to_all x1, waiting for transfers between devices: 3.34 us -> 2.09 us  [exchange(): lax.all_to_all(blocks, axis, 0, 0, tiled=True, axis_index_groups=[order])]
    all_to_all x1, blocking collectives: 13.8 us -> 13.1 us  [exchange(): lax.all_to_all(blocks, axis, 0, 0, tiled=True, axis_index_groups=[order])]
where the time goes in v4:
time: 48.2 us; the launch traced here: 47.9 us
  starting transfers between devices  22.5 us (47%)
  blocking collectives  13.1 us (27%)
  Pallas kernels  8.82 us (18%)
  waiting for transfers between devices  2.09 us (4%)
  between operations  1.34 us (3%)
    all_to_all x1, starting transfers between devices, exchange(): lax.all_to_all(blocks, axis, 0, 0, tiled=True, axis_index_groups=[order])  13.8 us
    all_to_all x1, blocking collectives, exchange(): lax.all_to_all(blocks, axis, 0, 0, tiled=True, axis_index_groups=[order])  13.1 us
    ppermute x1, starting transfers between devices, body(): lax.ppermute(send, 'bal', [(member, member ^ 1) for member in range(bal)])  8.79 us
    pallas_call x1, Pallas kernels, body(): pl.pallas_call(rows_kernel, out_shape=shape((count, width), jnp.bfloat16)...  3.05 us
    all_to_all x1, waiting for transfers between devices, exchange(): lax.all_to_all(blocks, axis, 0, 0, tiled=True, axis_index_groups=[order])  2.09 us
    pallas_call x1, Pallas kernels, body(): pl.pallas_call(prepare_kernel, out_shape=(shape((count, half + decoder),...  1.74 us
    pallas_call x1, Pallas kernels, body(): pl.pallas_call(own_kernel, out_shape=(shape((half, decoder), jnp.float32)...  1.74 us
    pallas_call x1, Pallas kernels, body(): pl.pallas_call(finish_kernel, out_shape=(shape((own, decoder), jnp.float3...  1.06 us
  transfers between devices with their start and end apart: 2, of which 1 were waited for; matrix products, arithmetic and copies ran while one was open for 0% of the time, Pallas kernels for 10%

profile of v4, /device:TPU:1, one launch (start us, length us, event | category | flops | bytes accessed | tf_op | source)
XLA Modules:
  0.0 47.9 jit_solution(17699359035717428102)
XLA Ops:
  1.3 1.7 %prepare.1 = (bf16[256,1024]{1,0:T(8,128)(2,1)S(1)}, bf16[2,256,512]{2,1,0:T(8,128)(2,1)S(1)}, f32[256,1024]{1,0:T(8,128)S(1)}, bf16[256,512]{1,0:T(8,128)(2,1)S(1)}) custom-call(s32[1]{0:T(128)S(6)} %copy.11.count_ref, bf16[256,1024]{1,0:T(8,128)(2,1)} %x_hbm.2, bf16[256,512]{1,0:T(8,128)(2,1)} %cot_hbm.2, f32[1,1024]{1,0:T(1,128)} %bitcast.5, ...), custom_call_target="tpu_custom_call" | custom-call | flops 5242880 | bytes 3000000 | tf_op jit(solution)/shard_map/prepare/pallas_call | solution.py:298
  3.0 8.8 %collective-permute-start = (bf16[256,1024]{1,0:T(8,128)(2,1)S(1)}, bf16[256,1024]{1,0:T(8,128)(2,1)S(1)}, u32[]{:S(2)}, u32[]{:S(2)}) collective-permute-start(bf16[256,1024]{1,0:T(8,128)(2,1)S(1)} %get-tuple-element.18), channel_id=1, source_target_pairs={{0,1},{1,0},{2,3},{3,2},{4,5},{5,4},{6,7},{7,6},{8,9},{9,8},{10,11... | collective-permute-start | bytes 1572872 | tf_op jit(solution)/shard_map/ppermute | solution.py:313
  11.8 1.7 %own.1 = (f32[512,512]{1,0:T(8,128)S(1)}, f32[16,128]{1,0:T(8,128)S(1)}) custom-call(s32[1]{0:T(128)S(6)} %copy.11.count_ref, bf16[2,256,512]{2,1,0:T(8,128)(2,1)S(1)} %get-tuple-element.19.hidden_ref, f32[256,1024]{1,0:T(8,128)S(1)} %get-tuple-element.20.normed_ref, bf16[256,512]{1,0:T(8,128)(2,1)S(1)} %get-tuple-element.21.live_ref, ...), custom_call_target="tpu_custom_call" | custom-call | flops 402653184 | bytes 3000000 | tf_op jit(solution)/shard_map/own/pallas_call | solution.py:314
  13.6 0.0 collective-permute-done.got_ref
  13.6 0.4 pair.1
  14.0 13.1 %all_to_all.10.got_ref = bf16[16,144,128]{2,1,0:T(8,128)(2,1)S(1)} all-to-all(bf16[16,144,128]{2,1,0:T(8,128)(2,1)S(1)} %pair.1), channel_id=1, replica_groups={{11,10,9,8,7,15,6,14,5,13,4,12,3,2,1,0},{27,26,25,24,23,31,22,30,21,29,..., dimensions={0} | all-to-all | bytes 1179648 | tf_op jit(solution)/shard_map/all_to_all | solution.py:280
  27.0 0.8 %regroup.1 = bf16[32,24,128]{2,1,0:T(8,128)(2,1)} custom-call(bf16[16,144,128]{2,1,0:T(8,128)(2,1)S(1)} %all_to_all.10.got_ref), custom_call_target="tpu_custom_call" | custom-call | flops 1000000 | bytes 1500000 | tf_op jit(solution)/shard_map/regroup/pallas_call | solution.py:338
  27.9 13.8 %all-to-all-start.1 = ((bf16[32,24,128]{2,1,0:T(8,128)(2,1)}), bf16[32,24,128]{2,1,0:T(8,128)(2,1)S(1)}, u32[]{:S(2)}, u32[]{:S(2)}) async-start(bf16[32,24,128]{2,1,0:T(8,128)(2,1)} %regroup.1), calls=%async_computation.1 | async-start | bytes 393216 | tf_op jit(solution)/shard_map/all_to_all | solution.py:280
  41.7 0.0 copy-start
  41.7 3.0 %rows.1 = bf16[256,1024]{1,0:T(8,128)(2,1)} custom-call(s32[1]{0:T(128)S(6)} %copy.11.count_ref, bf16[256,1024]{1,0:T(8,128)(2,1)} %x_hbm.2, bf16[256,512]{1,0:T(8,128)(2,1)} %cot_hbm.2, bf16[1024,512]{1,0:T(8,128)(2,1)} %projection_ref.1, f32[1,1024]{1,0:T(1,128)} %bitcast.6), custom_call_target="tpu_custom_call" | custom-call | flops 268435456 | bytes 3000000 | tf_op jit(solution)/shard_map/rows/pallas_call | solution.py:349
  44.7 2.1 %all-to-all-done.1.got_ref = bf16[32,24,128]{2,1,0:T(8,128)(2,1)S(1)} async-done(((bf16[32,24,128]{2,1,0:T(8,128)(2,1)}), bf16[32,24,128]{2,1,0:T(8,128)(2,1)S(1)}, u32[]{:S(2)}, u32[]{:S(2)}) %all-to-all-start.1) | async-done | bytes 196640 | tf_op jit(solution)/shard_map/all_to_all | solution.py:280
  46.8 0.0 copy-done
  46.8 1.1 %finish.1 = (f32[2,512]{1,0:T(2,128)}, f32[1,1024]{1,0:T(1,128)}, f32[1,1024]{1,0:T(1,128)}, f32[1,512]{1,0:T(1,128)}) custom-call(bf16[32,24,128]{2,1,0:T(8,128)(2,1)S(1)} %all-to-all-done.1.got_ref, bf16[1024,512]{1,0:T(8,128)(2,1)S(1)} %copy-done), custom_call_target="tpu_custom_call" | custom-call | flops 1000000 | bytes 300000 | tf_op jit(solution)/shard_map/finish/pallas_call | solution.py:361
Async XLA Ops:
  3.0 10.5 %collective-permute-start = (bf16[256,1024]{1,0:T(8,128)(2,1)S(1)}, bf16[256,1024]{1,0:T(8,128)(2,1)S(1)}, u32[]{:S(2)}, u32[]{:S(2)}) collective-permute-start(bf16[256,1024]{1,0:T(8,128)(2,1)S(1)} %get-tuple-element.18), channel_id=1, source_target_pairs={{0,1},{1,0},{2,3},{3,2},{4,5},{5,4},{6,7},{7,6},{8,9},{9,8},{10,11... | collective-permute-start | bytes 1572872 | tf_op jit(solution)/shard_map/ppermute | solution.py:313
  27.9 18.9 %all-to-all-start.1 = ((bf16[32,24,128]{2,1,0:T(8,128)(2,1)}), bf16[32,24,128]{2,1,0:T(8,128)(2,1)S(1)}, u32[]{:S(2)}, u32[]{:S(2)}) async-start(bf16[32,24,128]{2,1,0:T(8,128)(2,1)} %regroup.1), calls=%async_computation.1 | async-start | bytes 393216 | tf_op jit(solution)/shard_map/all_to_all | solution.py:280
  41.7 5.2 %copy-start = (bf16[1024,512]{1,0:T(8,128)(2,1)S(1)}, bf16[1024,512]{1,0:T(8,128)(2,1)}, u32[]{:S(2)}) copy-start(bf16[1024,512]{1,0:T(8,128)(2,1)} %projection_ref.1) | copy-start | bytes 3145732

commit v5 on v4

--- a/solution.py
+++ b/solution.py
@@ -11,6 +11,7 @@
 LANES = 128
 SUBLANES = 8
 CORES = 2
+PART_ROWS = 64
 COUNT_BASE = 256
 
 
@@ -94,49 +95,82 @@
     count_ref,
     x_hbm,
     cot_hbm,
+    weight_hbm,
     gain_hbm,
     beta_hbm,
     send_ref,
     hidden_ref,
     normed_ref,
-    live_ref,
+    inv_std_ref,
+    weight_ref,
     x_ref,
     cot_ref,
     gain_ref,
     beta_ref,
     arrived,
 ):
+    half = hidden_ref.shape[1]
     copies = start_copies(
         arrived,
         (x_hbm, x_ref),
         (gain_hbm, gain_ref),
         (beta_hbm, beta_ref),
         (cot_hbm, cot_ref),
-    )
-    half = hidden_ref.shape[2]
+        (weight_hbm, weight_ref),
+    )
+    first_core = lax.axis_index("bal") % CORES == 0
     copies[0].wait()
-    normed, _ = normalise(x_ref[...])
+    normed, inv_std = normalise(x_ref[...])
     normed_ref[...] = normed
-    for copy in copies[1:]:
+    inv_std_ref[...] = inv_std
+    for copy in copies[1:3]:
         copy.wait()
     hidden = (normed * gain_ref[...] + beta_ref[...]).astype(jnp.bfloat16)
-    for part in range(CORES):
-        hidden_ref[part] = hidden[:, part * half : (part + 1) * half]
-    cot_live = live_cotangent(count_ref, cot_ref)
-    live_ref[...] = cot_live
-    send_ref[:, half:] = cot_live
-    send_ref[:, :half] = hidden_ref[1 - lax.axis_index("bal") % CORES]
+    low, high = hidden[:, :half], hidden[:, half:]
+    hidden_ref[...] = jnp.where(first_core, low, high)
+    send_ref[:, :half] = jnp.where(first_core, high, low)
+    copies[3].wait()
+    send_ref[:, half:] = live_cotangent(count_ref, cot_ref)
+    copies[4].wait()
 
 
 def own_kernel(
-    count_ref, hidden_ref, normed_ref, live_ref, weight_hbm, product_ref, small, weight_ref, arrived
+    count_ref,
+    hidden_ref,
+    normed_ref,
+    inv_std_ref,
+    send_ref,
+    weight_ref,
+    gain_ref,
+    product_ref,
+    small,
+    rows_hbm,
+    rows_ref,
+    left,
 ):
-    copies = start_copies(arrived, (weight_hbm, weight_ref))
     width, decoder = weight_ref.shape
-    cot_live = live_ref[...]
-    product_ref[...] = project(hidden_ref[lax.axis_index("bal") % CORES], cot_live)
-    copies[0].wait()
+    cot_live = send_ref[:, hidden_ref.shape[1] :]
     grad_h = backproject(cot_live, weight_ref)
+    count = rows_ref.shape[0]
+    copies = []
+    for start in range(0, count, PART_ROWS):
+        part = slice(start, start + PART_ROWS)
+        normed = normed_ref[part]
+        scaled = grad_h[part] * gain_ref[...]
+        rows_ref[part] = (
+            inv_std_ref[part]
+            * (
+                scaled
+                - jnp.mean(scaled, axis=1, keepdims=True)
+                - normed * jnp.mean(scaled * normed, axis=1, keepdims=True)
+            )
+        ).astype(jnp.bfloat16)
+        copies.append(
+            pltpu.make_async_copy(
+                rows_ref.at[part], rows_hbm.at[part], left.at[start // PART_ROWS]
+            )
+        )
+        copies[-1].start()
     grad_gain = jnp.sum(grad_h * normed_ref[...], axis=0, keepdims=True)
     grad_bias = jnp.sum(cot_live.astype(jnp.float32), axis=0, keepdims=True)
     small[...] = jnp.zeros_like(small)
@@ -146,6 +180,9 @@
     small[at : at + 1] = count_row(
         jnp.full((1, 1), count_ref[0], jnp.int32).astype(jnp.float32)
     )
+    product_ref[...] = project(hidden_ref[...], cot_live)
+    for copy in copies:
+        copy.wait()
 
 
 def pair_kernel(dp, bal, own, got_ref, product_ref, small_ref, out_ref, grad_w):
@@ -221,41 +258,6 @@
     )
 
 
-def rows_kernel(
-    count_ref,
-    x_hbm,
-    cot_hbm,
-    weight_hbm,
-    gain_hbm,
-    out_ref,
-    x_ref,
-    cot_ref,
-    weight_ref,
-    gain_ref,
-    arrived,
-):
-    copies = start_copies(
-        arrived,
-        (x_hbm, x_ref),
-        (gain_hbm, gain_ref),
-        (cot_hbm, cot_ref),
-        (weight_hbm, weight_ref),
-    )
-    copies[0].wait()
-    normed, inv_std = normalise(x_ref[...])
-    for copy in copies[1:]:
-        copy.wait()
-    scaled = backproject(live_cotangent(count_ref, cot_ref), weight_ref) * gain_ref[...]
-    out_ref[...] = (
-        inv_std
-        * (
-            scaled
-            - jnp.mean(scaled, axis=1, keepdims=True)
-            - normed * jnp.mean(scaled * normed, axis=1, keepdims=True)
-        )
-    ).astype(jnp.bfloat16)
-
-
 VMEM = pl.BlockSpec(memory_space=pltpu.VMEM)
 SMEM = pl.BlockSpec(memory_space=pltpu.SMEM)
 HBM = pl.BlockSpec(memory_space=pltpu.HBM)
@@ -268,12 +270,6 @@
 
 def in_hbm(*arrays):
     return tuple(pltpu.with_memory_space_constraint(each, pltpu.HBM) for each in arrays)
-
-
-def scratch_of(*arrays):
-    return [pltpu.VMEM(each.shape, each.dtype) for each in arrays] + [
-        pltpu.SemaphoreType.DMA((len(arrays),))
-    ]
 
 
 def exchange(blocks, axis, order):
@@ -295,35 +291,46 @@
         beta = beta.reshape(1, width)
         work = 2 * count * width * decoder
         shape = jax.ShapeDtypeStruct
-        send, hidden, normed, live = pl.pallas_call(
+        send, hidden, normed, inv_std, weight_near = pl.pallas_call(
             prepare_kernel,
             out_shape=(
                 shape((count, half + decoder), jnp.bfloat16),
-                shape((CORES, count, half), jnp.bfloat16),
+                shape((count, half), jnp.bfloat16),
                 shape((count, width), jnp.float32),
-                shape((count, decoder), jnp.bfloat16),
+                shape((count, 1), jnp.float32),
+                shape(weight.shape, weight.dtype),
             ),
-            in_specs=[SMEM] + [HBM] * 4,
-            out_specs=(VMEM,) * 4,
-            scratch_shapes=scratch_of(rows, cotangent, gain, beta),
+            in_specs=[SMEM] + [HBM] * 5,
+            out_specs=(VMEM,) * 5,
+            scratch_shapes=[
+                pltpu.VMEM(rows.shape, rows.dtype),
+                pltpu.VMEM(cotangent.shape, cotangent.dtype),
+                pltpu.VMEM(gain.shape, gain.dtype),
+                pltpu.VMEM(beta.shape, beta.dtype),
+                pltpu.SemaphoreType.DMA((5,)),
+            ],
             compiler_params=PARAMS,
             cost_estimate=cost(20 * count * width, 3000000),
             name="prepare",
-        )(counts, *in_hbm(rows, cotangent, gain, beta))
+        )(counts, *in_hbm(rows, cotangent, weight, gain, beta))
         got = lax.ppermute(send, "bal", [(member, member ^ 1) for member in range(bal)])
-        product, small = pl.pallas_call(
+        product, small, grad_rows = pl.pallas_call(
             own_kernel,
             out_shape=(
                 shape((half, decoder), jnp.float32),
                 shape((kept, LANES), jnp.float32),
+                shape(rows.shape, rows.dtype),
             ),
-            in_specs=[SMEM] + [VMEM] * 3 + [HBM],
-            out_specs=(VMEM,) * 2,
-            scratch_shapes=scratch_of(weight),
+            in_specs=[SMEM] + [VMEM] * 6,
+            out_specs=(VMEM, VMEM, HBM),
+            scratch_shapes=[
+                pltpu.VMEM(rows.shape, rows.dtype),
+                pltpu.SemaphoreType.DMA((count // PART_ROWS,)),
+            ],
             compiler_params=PARAMS,
             cost_estimate=cost(3 * work // 2, 3000000),
             name="own",
-        )(counts, hidden, normed, live, *in_hbm(weight))
+        )(counts, hidden, normed, inv_std, send, weight_near, gain)
         first = pl.pallas_call(
             functools.partial(pair_kernel, dp, bal, own),
             out_shape=shape((bal, lines * peers + kept, LANES), jnp.bfloat16),
@@ -345,17 +352,6 @@
             cost_estimate=cost(1000000, 1500000),
             name="regroup",
         )(first)
-        second, rows, cotangent = lax.optimization_barrier((second, rows, cotangent))
-        grad_rows = pl.pallas_call(
-            rows_kernel,
-            out_shape=shape((count, width), jnp.bfloat16),
-            in_specs=[SMEM] + [HBM] * 4,
-            out_specs=VMEM,
-            scratch_shapes=scratch_of(rows, cotangent, weight, gain),
-            compiler_params=PARAMS,
-            cost_estimate=cost(work, 3000000),
-            name="rows",
-        )(counts, *in_hbm(rows, cotangent, weight, gain))
         second = exchange(second, "dp", dp_order(dp))
         vector = shape((1, width), jnp.float32)
         grad_weight, grad_gain, grad_beta, grad_bias = pl.pallas_call(
@@ -371,7 +367,7 @@
             compiler_params=PARAMS,
             cost_estimate=cost(1000000, 300000),
             name="finish",
-        )(second, weight)
+        )(second, weight_near)
         return (
             grad_rows,
             grad_weight,

time: 48.2 us -> 46.9 us (0.973)
  blocking collectives: 13.1 us -> 31.8 us
  starting transfers between devices: 22.5 us -> 8.79 us
  Pallas kernels: 8.82 us -> 4.7 us
  waiting for transfers between devices: 2.09 us -> 0.03 us
    all_to_all x1 -> x2, blocking collectives: 13.1 us -> 31.8 us  [exchange(): lax.all_to_all(blocks, axis, 0, 0, tiled=True, axis_index_groups=[order])]
    all_to_all x1 -> x0, starting transfers between devices: 13.8 us -> none  [exchange(): lax.all_to_all(blocks, axis, 0, 0, tiled=True, axis_index_groups=[order])]
    pallas_call x1 -> x0, Pallas kernels: 3.05 us -> none  [body(): pl.pallas_call(rows_kernel, out_shape=shape((count, width), jnp.bfloat16)...]
    all_to_all x1 -> x0, waiting for transfers between devices: 2.09 us -> none  [exchange(): lax.all_to_all(blocks, axis, 0, 0, tiled=True, axis_index_groups=[order])]
    pallas_call x1, Pallas kernels: 0.84 us -> 0.18 us  [body(): pl.pallas_call(functools.partial(regroup_kernel, dp, lines, at_count), ou...]
  transfers between devices with their start and end apart: 2 -> 1, of which waited for: 1 -> 0; matrix products, arithmetic and copies ran while one was open for 0% -> 0% of each run, Pallas kernels for 10% -> 3%
where the time goes in v5:
time: 46.9 us; the launch traced here: 46.6 us
  blocking collectives  31.8 us (68%)
  starting transfers between devices  8.79 us (19%)
  Pallas kernels  4.7 us (10%)
  between operations  1.33 us (3%)
    all_to_all x2, blocking collectives, exchange(): lax.all_to_all(blocks, axis, 0, 0, tiled=True, axis_index_groups=[order])  31.8 us
    ppermute x1, starting transfers between devices, body(): lax.ppermute(send, 'bal', [(member, member ^ 1) for member in range(bal)])  8.79 us
    pallas_call x1, Pallas kernels, body(): pl.pallas_call(prepare_kernel, out_shape=(shape((count, half + decoder),...  1.61 us
    pallas_call x1, Pallas kernels, body(): pl.pallas_call(own_kernel, out_shape=(shape((half, decoder), jnp.float32)...  1.47 us
    pallas_call x1, Pallas kernels, body(): pl.pallas_call(finish_kernel, out_shape=(shape((own, decoder), jnp.float3...  1.06 us
  transfers between devices with their start and end apart: 1, of which 0 were waited for; matrix products, arithmetic and copies ran while one was open for 0% of the time, Pallas kernels for 3%

profile of v5, /device:TPU:1, one launch (start us, length us, event | category | flops | bytes accessed | tf_op | source)
XLA Modules:
  0.0 46.6 jit_solution(10039826183521887863)
XLA Ops:
  1.3 1.6 %prepare.1 = (bf16[256,1024]{1,0:T(8,128)(2,1)S(1)}, bf16[256,512]{1,0:T(8,128)(2,1)S(1)}, f32[256,1024]{1,0:T(8,128)S(1)}, f32[256,1]{1,0:T(8,128)S(1)}, bf16[1024,512]{1,0:T(8,128)(2,1)S(1)}) custom-call(s32[1]{0:T(128)S(6)} %copy.11.count_ref, bf16[256,1024]{1,0:T(8,128)(2,1)} %x_hbm.1, bf16[256,512]{1,0:T(8,128)(2,1)} %cot_hbm.1, ...), custom_call_target="tpu_custom_call" | custom-call | flops 5242880 | bytes 3000000 | tf_op jit(solution)/shard_map/prepare/pallas_call | solution.py:294
  2.9 0.0 copy-start
  2.9 8.8 %collective-permute-start = (bf16[256,1024]{1,0:T(8,128)(2,1)S(1)}, bf16[256,1024]{1,0:T(8,128)(2,1)S(1)}, u32[]{:S(2)}, u32[]{:S(2)}) collective-permute-start(bf16[256,1024]{1,0:T(8,128)(2,1)S(1)} %get-tuple-element.20.send_ref), channel_id=1, source_target_pairs={{0,1},{1,0},{2,3},{3,2},{4,5},{5,4},{6,7},{7,6},{8,9},{9,8},{10,11... | collective-permute-start | bytes 1572872 | tf_op jit(solution)/shard_map/ppermute | solution.py:316
  11.7 0.0 copy-done
  11.7 1.5 %own.1 = (f32[512,512]{1,0:T(8,128)S(1)}, f32[16,128]{1,0:T(8,128)S(1)}, bf16[256,1024]{1,0:T(8,128)(2,1)}) custom-call(s32[1]{0:T(128)S(6)} %copy.11.count_ref, bf16[256,512]{1,0:T(8,128)(2,1)S(1)} %get-tuple-element.17.hidden_ref, f32[256,1024]{1,0:T(8,128)S(1)} %get-tuple-element.18.normed_ref, f32[256,1]{1,0:T(8,128)S(1)} %get-tuple-element.19.inv_std_ref, ...), custom_call_target="tpu_custom_call" | custom-call | flops 402653184 | bytes 3000000 | tf_op jit(solution)/shard_map/own/pallas_call | solution.py:317
  13.2 0.0 collective-permute-done.got_ref
  13.2 0.4 pair.1
  13.6 13.3 %all_to_all.10.got_ref = bf16[16,144,128]{2,1,0:T(8,128)(2,1)S(1)} all-to-all(bf16[16,144,128]{2,1,0:T(8,128)(2,1)S(1)} %pair.1), channel_id=1, replica_groups={{11,10,9,8,7,15,6,14,5,13,4,12,3,2,1,0},{27,26,25,24,23,31,22,30,21,29,..., dimensions={0} | all-to-all | bytes 1179648 | tf_op jit(solution)/shard_map/all_to_all | solution.py:276
  26.9 0.2 regroup.1
  27.1 18.5 %all_to_all.11.got_ref = bf16[32,24,128]{2,1,0:T(8,128)(2,1)S(1)} all-to-all(bf16[32,24,128]{2,1,0:T(8,128)(2,1)S(1)} %regroup.1), channel_id=1, replica_groups={{288,224,352,160,272,304,416,96,208,240,336,368,480,32,144,176,256,400,..., dimensions={0} | all-to-all | bytes 393216 | tf_op jit(solution)/shard_map/all_to_all | solution.py:276
  45.6 1.1 %finish.1 = (f32[2,512]{1,0:T(2,128)}, f32[1,1024]{1,0:T(1,128)}, f32[1,1024]{1,0:T(1,128)}, f32[1,512]{1,0:T(1,128)}) custom-call(bf16[32,24,128]{2,1,0:T(8,128)(2,1)S(1)} %all_to_all.11.got_ref, bf16[1024,512]{1,0:T(8,128)(2,1)S(1)} %get-tuple-element.21.weight_ref.projection_ref), custom_call_target="tpu_custom_call" | custom-call | flops 1000000 | bytes 300000 | tf_op jit(solution)/shard_map/finish/pallas_call | solution.py:357
Async XLA Ops:
  2.9 8.8 %copy-start = (f32[1024]{0:T(1024)S(1)}, f32[1024]{0:T(1024)}, u32[]{:S(2)}) copy-start(f32[1024]{0:T(1024)} %param.10) | copy-start | bytes 12292
  2.9 10.3 %collective-permute-start = (bf16[256,1024]{1,0:T(8,128)(2,1)S(1)}, bf16[256,1024]{1,0:T(8,128)(2,1)S(1)}, u32[]{:S(2)}, u32[]{:S(2)}) collective-permute-start(bf16[256,1024]{1,0:T(8,128)(2,1)S(1)} %get-tuple-element.20.send_ref), channel_id=1, source_target_pairs={{0,1},{1,0},{2,3},{3,2},{4,5},{5,4},{6,7},{7,6},{8,9},{9,8},{10,11... | collective-permute-start | bytes 1572872 | tf_op jit(solution)/shard_map/ppermute | solution.py:316

commit v6 on v5

--- a/solution.py
+++ b/solution.py
@@ -336,7 +336,7 @@
             out_shape=shape((bal, lines * peers + kept, LANES), jnp.bfloat16),
             in_specs=[VMEM] * 3,
             out_specs=VMEM,
-            scratch_shapes=[pltpu.VMEM((tiles, peers * (bal * own + 1), LANES), jnp.float32)],
+            scratch_shapes=[pltpu.VMEM((tiles, (peers + 1) * (bal * own + 1), LANES), jnp.float32)],
             compiler_params=PARAMS,
             cost_estimate=cost(work // 2, 2000000),
             name="pair",
@@ -347,7 +347,7 @@
             out_shape=shape((dp, lines + kept, LANES), jnp.bfloat16),
             in_specs=[VMEM],
             out_specs=VMEM,
-            scratch_shapes=[pltpu.VMEM((dp * lines, LANES), jnp.float32)],
+            scratch_shapes=[pltpu.VMEM(((dp + 1) * lines, LANES), jnp.float32)],
             compiler_params=PARAMS,
             cost_estimate=cost(1000000, 1500000),
             name="regroup",

time: 46.9 us -> 46.9 us (level)
  no operation moved by 1% of the time
where the time goes in v6:
time: 46.9 us; the launch traced here: 46.6 us
  blocking collectives  31.8 us (68%)
  starting transfers between devices  8.79 us (19%)
  Pallas kernels  4.7 us (10%)
  between operations  1.33 us (3%)
    all_to_all x2, blocking collectives, exchange(): lax.all_to_all(blocks, axis, 0, 0, tiled=True, axis_index_groups=[order])  31.8 us
    ppermute x1, starting transfers between devices, body(): lax.ppermute(send, 'bal', [(member, member ^ 1) for member in range(bal)])  8.79 us
    pallas_call x1, Pallas kernels, body(): pl.pallas_call(prepare_kernel, out_shape=(shape((count, half + decoder),...  1.61 us
    pallas_call x1, Pallas kernels, body(): pl.pallas_call(own_kernel, out_shape=(shape((half, decoder), jnp.float32)...  1.47 us
    pallas_call x1, Pallas kernels, body(): pl.pallas_call(finish_kernel, out_shape=(shape((own, decoder), jnp.float3...  1.06 us
  transfers between devices with their start and end apart: 1, of which 0 were waited for; matrix products, arithmetic and copies ran while one was open for 0% of the time, Pallas kernels for 3%

profile of v6, /device:TPU:1, one launch (start us, length us, event | category | flops | bytes accessed | tf_op | source)
XLA Modules:
  0.0 46.6 jit_solution(816072336753516885)
XLA Ops:
  1.3 1.6 %prepare.1 = (bf16[256,1024]{1,0:T(8,128)(2,1)S(1)}, bf16[256,512]{1,0:T(8,128)(2,1)S(1)}, f32[256,1024]{1,0:T(8,128)S(1)}, f32[256,1]{1,0:T(8,128)S(1)}, bf16[1024,512]{1,0:T(8,128)(2,1)S(1)}) custom-call(s32[1]{0:T(128)S(6)} %copy.11.count_ref, bf16[256,1024]{1,0:T(8,128)(2,1)} %x_hbm.1, bf16[256,512]{1,0:T(8,128)(2,1)} %cot_hbm.1, ...), custom_call_target="tpu_custom_call" | custom-call | flops 5242880 | bytes 3000000 | tf_op jit(solution)/shard_map/prepare/pallas_call | solution.py:294
  2.9 0.0 copy-start
  2.9 8.8 %collective-permute-start = (bf16[256,1024]{1,0:T(8,128)(2,1)S(1)}, bf16[256,1024]{1,0:T(8,128)(2,1)S(1)}, u32[]{:S(2)}, u32[]{:S(2)}) collective-permute-start(bf16[256,1024]{1,0:T(8,128)(2,1)S(1)} %get-tuple-element.20.send_ref), channel_id=1, source_target_pairs={{0,1},{1,0},{2,3},{3,2},{4,5},{5,4},{6,7},{7,6},{8,9},{9,8},{10,11... | collective-permute-start | bytes 1572872 | tf_op jit(solution)/shard_map/ppermute | solution.py:316
  11.7 0.0 copy-done
  11.7 1.5 %own.1 = (f32[512,512]{1,0:T(8,128)S(1)}, f32[16,128]{1,0:T(8,128)S(1)}, bf16[256,1024]{1,0:T(8,128)(2,1)}) custom-call(s32[1]{0:T(128)S(6)} %copy.11.count_ref, bf16[256,512]{1,0:T(8,128)(2,1)S(1)} %get-tuple-element.17.hidden_ref, f32[256,1024]{1,0:T(8,128)S(1)} %get-tuple-element.18.normed_ref, f32[256,1]{1,0:T(8,128)S(1)} %get-tuple-element.19.inv_std_ref, ...), custom_call_target="tpu_custom_call" | custom-call | flops 402653184 | bytes 3000000 | tf_op jit(solution)/shard_map/own/pallas_call | solution.py:317
  13.2 0.0 collective-permute-done.got_ref
  13.2 0.4 pair.1
  13.6 13.3 %all_to_all.10.got_ref = bf16[16,144,128]{2,1,0:T(8,128)(2,1)S(1)} all-to-all(bf16[16,144,128]{2,1,0:T(8,128)(2,1)S(1)} %pair.1), channel_id=1, replica_groups={{11,10,9,8,7,15,6,14,5,13,4,12,3,2,1,0},{27,26,25,24,23,31,22,30,21,29,..., dimensions={0} | all-to-all | bytes 1179648 | tf_op jit(solution)/shard_map/all_to_all | solution.py:276
  26.9 0.2 regroup.1
  27.1 18.5 %all_to_all.11.got_ref = bf16[32,24,128]{2,1,0:T(8,128)(2,1)S(1)} all-to-all(bf16[32,24,128]{2,1,0:T(8,128)(2,1)S(1)} %regroup.1), channel_id=1, replica_groups={{288,224,352,160,272,304,416,96,208,240,336,368,480,32,144,176,256,400,..., dimensions={0} | all-to-all | bytes 393216 | tf_op jit(solution)/shard_map/all_to_all | solution.py:276
  45.6 1.1 %finish.1 = (f32[2,512]{1,0:T(2,128)}, f32[1,1024]{1,0:T(1,128)}, f32[1,1024]{1,0:T(1,128)}, f32[1,512]{1,0:T(1,128)}) custom-call(bf16[32,24,128]{2,1,0:T(8,128)(2,1)S(1)} %all_to_all.11.got_ref, bf16[1024,512]{1,0:T(8,128)(2,1)S(1)} %get-tuple-element.21.weight_ref.projection_ref), custom_call_target="tpu_custom_call" | custom-call | flops 1000000 | bytes 300000 | tf_op jit(solution)/shard_map/finish/pallas_call | solution.py:357
Async XLA Ops:
  2.9 8.8 %copy-start = (f32[1024]{0:T(1024)S(1)}, f32[1024]{0:T(1024)}, u32[]{:S(2)}) copy-start(f32[1024]{0:T(1024)} %param.10) | copy-start | bytes 12292
  2.9 10.3 %collective-permute-start = (bf16[256,1024]{1,0:T(8,128)(2,1)S(1)}, bf16[256,1024]{1,0:T(8,128)(2,1)S(1)}, u32[]{:S(2)}, u32[]{:S(2)}) collective-permute-start(bf16[256,1024]{1,0:T(8,128)(2,1)S(1)} %get-tuple-element.20.send_ref), channel_id=1, source_target_pairs={{0,1},{1,0},{2,3},{3,2},{4,5},{5,4},{6,7},{7,6},{8,9},{9,8},{10,11... | collective-permute-start | bytes 1572872 | tf_op jit(solution)/shard_map/ppermute | solution.py:316

commit v7 on v6

--- a/solution.py
+++ b/solution.py
@@ -217,15 +217,15 @@
     small = sum(part[lines * peers :] for part in halves)
     line = lax.broadcasted_iota(jnp.int32, small.shape, 0)
     count = count_of(small[at_count : at_count + 1])
-    small = jnp.where(line == at_count, count_row(count), small).astype(jnp.bfloat16)
+    small = jnp.where(line == at_count, count_row(count), small)
     for core in range(CORES):
         for row in range(lines):
             spread[pl.ds(core * peers * lines + row, peers, stride=lines), :] = halves[core][
                 row * peers : (row + 1) * peers
             ]
     for place, peer in enumerate(dp_order(dp)):
-        out_ref[place, :lines, :] = spread[peer * lines : (peer + 1) * lines].astype(jnp.bfloat16)
-        out_ref[place, lines:, :] = small
+        block = [spread[peer * lines : (peer + 1) * lines], small]
+        out_ref[place] = jnp.concatenate(block, axis=0).astype(jnp.bfloat16)
 
 
 def finish_kernel(got_ref, projection_ref, weight_ref, gain_ref, beta_ref, bias_ref):
@@ -235,27 +235,29 @@
     at_gain = own * tiles
     at_bias = at_gain + width // LANES
     at_count = at_bias + tiles
-    scaled = total * lax.rsqrt(count_of(total[at_count : at_count + 1]))
 
     def joined(start, lines):
         return jnp.concatenate(
-            [scaled[start + line : start + line + 1] for line in range(lines)], axis=1
+            [total[start + line : start + line + 1] for line in range(lines)], axis=1
         )
 
-    for tile in range(tiles):
-        weight_ref[:, tile * LANES : (tile + 1) * LANES] = scaled[tile * own : (tile + 1) * own]
-    gain_ref[...] = joined(at_gain, width // LANES)
     bias = joined(at_bias, tiles)
-    bias_ref[...] = bias
+    rest = bias
     row = lax.broadcasted_iota(jnp.int32, (SUBLANES, decoder), 0)
     terms = jnp.zeros((SUBLANES, decoder), jnp.float32)
     for term in range(3):
-        part = bias.astype(jnp.bfloat16).astype(jnp.float32)
+        part = rest.astype(jnp.bfloat16).astype(jnp.float32)
         terms = jnp.where(row == term, part, terms)
-        bias = bias - part
-    beta_ref[...] = jnp.sum(
-        backproject(terms.astype(jnp.bfloat16), projection_ref), axis=0, keepdims=True
-    )
+        rest = rest - part
+    beta = backproject(terms.astype(jnp.bfloat16), projection_ref)
+    scale = lax.rsqrt(count_of(total[at_count : at_count + 1]))
+    for tile in range(tiles):
+        weight_ref[:, tile * LANES : (tile + 1) * LANES] = (
+            total[tile * own : (tile + 1) * own] * scale
+        )
+    gain_ref[...] = joined(at_gain, width // LANES) * scale
+    bias_ref[...] = bias * scale
+    beta_ref[...] = jnp.sum(beta, axis=0, keepdims=True) * scale
 
 
 VMEM = pl.BlockSpec(memory_space=pltpu.VMEM)

time: 46.9 us -> 46.8 us (level)
  no operation moved by 1% of the time
where the time goes in v7:
time: 46.8 us; the launch traced here: 46.6 us
  blocking collectives  31.8 us (68%)
  starting transfers between devices  8.79 us (19%)
  Pallas kernels  4.64 us (10%)
  between operations  1.33 us (3%)
    all_to_all x2, blocking collectives, exchange(): lax.all_to_all(blocks, axis, 0, 0, tiled=True, axis_index_groups=[order])  31.8 us
    ppermute x1, starting transfers between devices, body(): lax.ppermute(send, 'bal', [(member, member ^ 1) for member in range(bal)])  8.79 us
    pallas_call x1, Pallas kernels, body(): pl.pallas_call(prepare_kernel, out_shape=(shape((count, half + decoder),...  1.61 us
    pallas_call x1, Pallas kernels, body(): pl.pallas_call(own_kernel, out_shape=(shape((half, decoder), jnp.float32)...  1.47 us
    pallas_call x1, Pallas kernels, body(): pl.pallas_call(finish_kernel, out_shape=(shape((own, decoder), jnp.float3...  1 us
  transfers between devices with their start and end apart: 1, of which 0 were waited for; matrix products, arithmetic and copies ran while one was open for 0% of the time, Pallas kernels for 3%

profile of v7, /device:TPU:1, one launch (start us, length us, event | category | flops | bytes accessed | tf_op | source)
XLA Modules:
  0.0 46.6 jit_solution(6215745319925468904)
XLA Ops:
  1.3 1.6 %prepare.1 = (bf16[256,1024]{1,0:T(8,128)(2,1)S(1)}, bf16[256,512]{1,0:T(8,128)(2,1)S(1)}, f32[256,1024]{1,0:T(8,128)S(1)}, f32[256,1]{1,0:T(8,128)S(1)}, bf16[1024,512]{1,0:T(8,128)(2,1)S(1)}) custom-call(s32[1]{0:T(128)S(6)} %copy.11.count_ref, bf16[256,1024]{1,0:T(8,128)(2,1)} %x_hbm.1, bf16[256,512]{1,0:T(8,128)(2,1)} %cot_hbm.1, ...), custom_call_target="tpu_custom_call" | custom-call | flops 5242880 | bytes 3000000 | tf_op jit(solution)/shard_map/prepare/pallas_call | solution.py:296
  2.9 0.0 copy-start
  2.9 8.8 %collective-permute-start = (bf16[256,1024]{1,0:T(8,128)(2,1)S(1)}, bf16[256,1024]{1,0:T(8,128)(2,1)S(1)}, u32[]{:S(2)}, u32[]{:S(2)}) collective-permute-start(bf16[256,1024]{1,0:T(8,128)(2,1)S(1)} %get-tuple-element.20.send_ref), channel_id=1, source_target_pairs={{0,1},{1,0},{2,3},{3,2},{4,5},{5,4},{6,7},{7,6},{8,9},{9,8},{10,11... | collective-permute-start | bytes 1572872 | tf_op jit(solution)/shard_map/ppermute | solution.py:318
  11.7 0.0 copy-done
  11.7 1.5 %own.1 = (f32[512,512]{1,0:T(8,128)S(1)}, f32[16,128]{1,0:T(8,128)S(1)}, bf16[256,1024]{1,0:T(8,128)(2,1)}) custom-call(s32[1]{0:T(128)S(6)} %copy.11.count_ref, bf16[256,512]{1,0:T(8,128)(2,1)S(1)} %get-tuple-element.17.hidden_ref, f32[256,1024]{1,0:T(8,128)S(1)} %get-tuple-element.18.normed_ref, f32[256,1]{1,0:T(8,128)S(1)} %get-tuple-element.19.inv_std_ref, ...), custom_call_target="tpu_custom_call" | custom-call | flops 402653184 | bytes 3000000 | tf_op jit(solution)/shard_map/own/pallas_call | solution.py:319
  13.2 0.0 collective-permute-done.got_ref
  13.2 0.4 pair.1
  13.6 13.3 %all_to_all.10.got_ref = bf16[16,144,128]{2,1,0:T(8,128)(2,1)S(1)} all-to-all(bf16[16,144,128]{2,1,0:T(8,128)(2,1)S(1)} %pair.1), channel_id=1, replica_groups={{11,10,9,8,7,15,6,14,5,13,4,12,3,2,1,0},{27,26,25,24,23,31,22,30,21,29,..., dimensions={0} | all-to-all | bytes 1179648 | tf_op jit(solution)/shard_map/all_to_all | solution.py:278
  26.9 0.2 regroup.1
  27.1 18.5 %all_to_all.11.got_ref = bf16[32,24,128]{2,1,0:T(8,128)(2,1)S(1)} all-to-all(bf16[32,24,128]{2,1,0:T(8,128)(2,1)S(1)} %regroup.1), channel_id=1, replica_groups={{288,224,352,160,272,304,416,96,208,240,336,368,480,32,144,176,256,400,..., dimensions={0} | all-to-all | bytes 393216 | tf_op jit(solution)/shard_map/all_to_all | solution.py:278
  45.6 1.0 %finish.1 = (f32[2,512]{1,0:T(2,128)}, f32[1,1024]{1,0:T(1,128)}, f32[1,1024]{1,0:T(1,128)}, f32[1,512]{1,0:T(1,128)}) custom-call(bf16[32,24,128]{2,1,0:T(8,128)(2,1)S(1)} %all_to_all.11.got_ref, bf16[1024,512]{1,0:T(8,128)(2,1)S(1)} %get-tuple-element.21.weight_ref.projection_ref), custom_call_target="tpu_custom_call" | custom-call | flops 1000000 | bytes 300000 | tf_op jit(solution)/shard_map/finish/pallas_call | solution.py:359
Async XLA Ops:
  2.9 8.8 %copy-start = (f32[1024]{0:T(1024)S(1)}, f32[1024]{0:T(1024)}, u32[]{:S(2)}) copy-start(f32[1024]{0:T(1024)} %param.10) | copy-start | bytes 12292
  2.9 10.3 %collective-permute-start = (bf16[256,1024]{1,0:T(8,128)(2,1)S(1)}, bf16[256,1024]{1,0:T(8,128)(2,1)S(1)}, u32[]{:S(2)}, u32[]{:S(2)}) collective-permute-start(bf16[256,1024]{1,0:T(8,128)(2,1)S(1)} %get-tuple-element.20.send_ref), channel_id=1, source_target_pairs={{0,1},{1,0},{2,3},{3,2},{4,5},{5,4},{6,7},{7,6},{8,9},{9,8},{10,11... | collective-permute-start | bytes 1572872 | tf_op jit(solution)/shard_map/ppermute | solution.py:318

commit v8 on v7

--- a/solution.py
+++ b/solution.py
@@ -15,24 +15,14 @@
 COUNT_BASE = 256
 
 
-def ring(step, size):
-    return min(step % size, -step % size)
-
-
 def bal_order(bal):
-    return sorted(
-        range(bal), key=lambda at: (-2 * ring(at // 4, bal // 4) - at // 2 % 2 - 0.5 * (at % 2), at)
-    )
+    far = 3 * bal // 4 - 1
+    return [far] + [at for at in range(bal) if at != far]
 
 
 def dp_order(dp):
-    size_y, size_z = dp // 4, 4
-    start = (size_y // 2, size_z // 2)
-
-    def distance(at):
-        return ring(at // size_z - start[0], size_y) + 2 * ring(at % size_z - start[1], size_z)
-
-    return sorted(range(dp), key=lambda at: (distance(at), at))
+    far = dp // 2 + 2
+    return [far] + [at for at in range(dp) if at != far]
 
 
 def normalise(x_rows):
@@ -112,25 +102,25 @@
     half = hidden_ref.shape[1]
     copies = start_copies(
         arrived,
+        (cot_hbm, cot_ref),
         (x_hbm, x_ref),
         (gain_hbm, gain_ref),
         (beta_hbm, beta_ref),
-        (cot_hbm, cot_ref),
         (weight_hbm, weight_ref),
     )
     first_core = lax.axis_index("bal") % CORES == 0
     copies[0].wait()
+    send_ref[:, half:] = live_cotangent(count_ref, cot_ref)
+    copies[1].wait()
     normed, inv_std = normalise(x_ref[...])
     normed_ref[...] = normed
     inv_std_ref[...] = inv_std
-    for copy in copies[1:3]:
+    for copy in copies[2:4]:
         copy.wait()
     hidden = (normed * gain_ref[...] + beta_ref[...]).astype(jnp.bfloat16)
     low, high = hidden[:, :half], hidden[:, half:]
     hidden_ref[...] = jnp.where(first_core, low, high)
     send_ref[:, :half] = jnp.where(first_core, high, low)
-    copies[3].wait()
-    send_ref[:, half:] = live_cotangent(count_ref, cot_ref)
     copies[4].wait()
 
 

time: 46.8 us -> 46.6 us (level)
  no operation moved by 1% of the time
where the time goes in v8:
time: 46.6 us; the launch traced here: 46.3 us
  blocking collectives  31.5 us (68%)
  starting transfers between devices  8.79 us (19%)
  Pallas kernels  4.69 us (10%)
  between operations  1.33 us (3%)
    all_to_all x2, blocking collectives, exchange(): lax.all_to_all(blocks, axis, 0, 0, tiled=True, axis_index_groups=[order])  31.5 us
    ppermute x1, starting transfers between devices, body(): lax.ppermute(send, 'bal', [(member, member ^ 1) for member in range(bal)])  8.79 us
    pallas_call x1, Pallas kernels, body(): pl.pallas_call(prepare_kernel, out_shape=(shape((count, half + decoder),...  1.67 us
    pallas_call x1, Pallas kernels, body(): pl.pallas_call(own_kernel, out_shape=(shape((half, decoder), jnp.float32)...  1.47 us
    pallas_call x1, Pallas kernels, body(): pl.pallas_call(finish_kernel, out_shape=(shape((own, decoder), jnp.float3...  1 us
  transfers between devices with their start and end apart: 1, of which 0 were waited for; matrix products, arithmetic and copies ran while one was open for 0% of the time, Pallas kernels for 3%

profile of v8, /device:TPU:1, one launch (start us, length us, event | category | flops | bytes accessed | tf_op | source)
XLA Modules:
  0.0 46.3 jit_solution(12144346958910402283)
XLA Ops:
  1.3 1.7 %prepare.1 = (bf16[256,1024]{1,0:T(8,128)(2,1)S(1)}, bf16[256,512]{1,0:T(8,128)(2,1)S(1)}, f32[256,1024]{1,0:T(8,128)S(1)}, f32[256,1]{1,0:T(8,128)S(1)}, bf16[1024,512]{1,0:T(8,128)(2,1)S(1)}) custom-call(s32[1]{0:T(128)S(6)} %copy.11.count_ref, bf16[256,1024]{1,0:T(8,128)(2,1)} %x_hbm.1, bf16[256,512]{1,0:T(8,128)(2,1)} %cot_hbm.1, ...), custom_call_target="tpu_custom_call" | custom-call | flops 5242880 | bytes 3000000 | tf_op jit(solution)/shard_map/prepare/pallas_call | solution.py:286
  3.0 0.0 copy-start
  3.0 8.8 %collective-permute-start = (bf16[256,1024]{1,0:T(8,128)(2,1)S(1)}, bf16[256,1024]{1,0:T(8,128)(2,1)S(1)}, u32[]{:S(2)}, u32[]{:S(2)}) collective-permute-start(bf16[256,1024]{1,0:T(8,128)(2,1)S(1)} %get-tuple-element.20.send_ref), channel_id=1, source_target_pairs={{0,1},{1,0},{2,3},{3,2},{4,5},{5,4},{6,7},{7,6},{8,9},{9,8},{10,11... | collective-permute-start | bytes 1572872 | tf_op jit(solution)/shard_map/ppermute | solution.py:308
  11.8 0.0 copy-done
  11.8 1.5 %own.1 = (f32[512,512]{1,0:T(8,128)S(1)}, f32[16,128]{1,0:T(8,128)S(1)}, bf16[256,1024]{1,0:T(8,128)(2,1)}) custom-call(s32[1]{0:T(128)S(6)} %copy.11.count_ref, bf16[256,512]{1,0:T(8,128)(2,1)S(1)} %get-tuple-element.17.hidden_ref, f32[256,1024]{1,0:T(8,128)S(1)} %get-tuple-element.18.normed_ref, f32[256,1]{1,0:T(8,128)S(1)} %get-tuple-element.19.inv_std_ref, ...), custom_call_target="tpu_custom_call" | custom-call | flops 402653184 | bytes 3000000 | tf_op jit(solution)/shard_map/own/pallas_call | solution.py:309
  13.2 0.0 collective-permute-done.got_ref
  13.3 0.4 pair.1
  13.7 13.2 %all_to_all.10.got_ref = bf16[16,144,128]{2,1,0:T(8,128)(2,1)S(1)} all-to-all(bf16[16,144,128]{2,1,0:T(8,128)(2,1)S(1)} %pair.1), channel_id=1, replica_groups={{11,0,1,2,3,4,5,6,7,8,9,10,12,13,14,15},{27,16,17,18,19,20,21,22,23,24,..., dimensions={0} | all-to-all | bytes 1179648 | tf_op jit(solution)/shard_map/all_to_all | solution.py:268
  26.9 0.2 regroup.1
  27.1 18.3 %all_to_all.11.got_ref = bf16[32,24,128]{2,1,0:T(8,128)(2,1)S(1)} all-to-all(bf16[32,24,128]{2,1,0:T(8,128)(2,1)S(1)} %regroup.1), channel_id=1, replica_groups={{288,0,16,32,48,64,80,96,112,128,144,160,176,192,208,224,240,256,272,30..., dimensions={0} | all-to-all | bytes 393216 | tf_op jit(solution)/shard_map/all_to_all | solution.py:268
  45.3 1.0 %finish.1 = (f32[2,512]{1,0:T(2,128)}, f32[1,1024]{1,0:T(1,128)}, f32[1,1024]{1,0:T(1,128)}, f32[1,512]{1,0:T(1,128)}) custom-call(bf16[32,24,128]{2,1,0:T(8,128)(2,1)S(1)} %all_to_all.11.got_ref, bf16[1024,512]{1,0:T(8,128)(2,1)S(1)} %get-tuple-element.21.weight_ref.projection_ref), custom_call_target="tpu_custom_call" | custom-call | flops 1000000 | bytes 300000 | tf_op jit(solution)/shard_map/finish/pallas_call | solution.py:349
Async XLA Ops:
  3.0 8.8 %copy-start = (f32[1024]{0:T(1024)S(1)}, f32[1024]{0:T(1024)}, u32[]{:S(2)}) copy-start(f32[1024]{0:T(1024)} %param.10) | copy-start | bytes 12292
  3.0 10.3 %collective-permute-start = (bf16[256,1024]{1,0:T(8,128)(2,1)S(1)}, bf16[256,1024]{1,0:T(8,128)(2,1)S(1)}, u32[]{:S(2)}, u32[]{:S(2)}) collective-permute-start(bf16[256,1024]{1,0:T(8,128)(2,1)S(1)} %get-tuple-element.20.send_ref), channel_id=1, source_target_pairs={{0,1},{1,0},{2,3},{3,2},{4,5},{5,4},{6,7},{7,6},{8,9},{9,8},{10,11... | collective-permute-start | bytes 1572872 | tf_op jit(solution)/shard_map/ppermute | solution.py:308

commit v9 on v8

--- a/solution.py
+++ b/solution.py
@@ -180,22 +180,29 @@
     pitch = span + 1
     peers = dp // CORES
     half, decoder = product_ref.shape
-    product = product_ref[...] + project(got_ref[:, :half], got_ref[:, half:])
-    for tile in range(decoder // LANES):
-        at = slice(tile * LANES, (tile + 1) * LANES)
-        for peer in range(peers):
-            grad_w[tile, peer * pitch : peer * pitch + span] = product[
-                peer * span : (peer + 1) * span, at
-            ]
+    tiles = decoder // LANES
     small = small_ref[...].astype(jnp.bfloat16)
-    tiles = decoder // LANES
-    for place, owner in enumerate(bal_order(bal)):
-        for tile in range(tiles):
-            for row in range(own):
-                rows = pl.ds(owner * own + row, peers, stride=pitch)
-                at = (tile * own + row) * peers
-                out_ref[place, at : at + peers, :] = grad_w[tile, rows, :].astype(jnp.bfloat16)
+    order = bal_order(bal)
+    for place in range(bal):
         out_ref[place, tiles * own * peers :, :] = small
+    hidden = got_ref[:, :half]
+    for first in range(0, tiles, 2):
+        at = slice(first * LANES, (first + 2) * LANES)
+        cot_live = got_ref[:, half + first * LANES : half + (first + 2) * LANES]
+        product = product_ref[:, at] + project(hidden, cot_live)
+        for tile in (first, first + 1):
+            at = slice((tile - first) * LANES, (tile - first + 1) * LANES)
+            for peer in range(peers):
+                grad_w[tile, peer * pitch : peer * pitch + span] = product[
+                    peer * span : (peer + 1) * span, at
+                ]
+            for place, owner in enumerate(order):
+                for row in range(own):
+                    rows = pl.ds(owner * own + row, peers, stride=pitch)
+                    at_row = (tile * own + row) * peers
+                    out_ref[place, at_row : at_row + peers, :] = grad_w[tile, rows, :].astype(
+                        jnp.bfloat16
+                    )
 
 
 def regroup_kernel(dp, lines, at_count, got_ref, out_ref, spread):

time: 46.6 us -> 46.6 us (level)
  no operation moved by 1% of the time
where the time goes in v9:
time: 46.6 us; the launch traced here: 46.3 us
  blocking collectives  31.5 us (68%)
  starting transfers between devices  8.79 us (19%)
  Pallas kernels  4.69 us (10%)
  between operations  1.33 us (3%)
    all_to_all x2, blocking collectives, exchange(): lax.all_to_all(blocks, axis, 0, 0, tiled=True, axis_index_groups=[order])  31.5 us
    ppermute x1, starting transfers between devices, body(): lax.ppermute(send, 'bal', [(member, member ^ 1) for member in range(bal)])  8.79 us
    pallas_call x1, Pallas kernels, body(): pl.pallas_call(prepare_kernel, out_shape=(shape((count, half + decoder),...  1.67 us
    pallas_call x1, Pallas kernels, body(): pl.pallas_call(own_kernel, out_shape=(shape((half, decoder), jnp.float32)...  1.47 us
    pallas_call x1, Pallas kernels, body(): pl.pallas_call(finish_kernel, out_shape=(shape((own, decoder), jnp.float3...  1 us
  transfers between devices with their start and end apart: 1, of which 0 were waited for; matrix products, arithmetic and copies ran while one was open for 0% of the time, Pallas kernels for 3%

profile of v9, /device:TPU:1, one launch (start us, length us, event | category | flops | bytes accessed | tf_op | source)
XLA Modules:
  0.0 46.3 jit_solution(1782585520706063672)
XLA Ops:
  1.3 1.7 %prepare.1 = (bf16[256,1024]{1,0:T(8,128)(2,1)S(1)}, bf16[256,512]{1,0:T(8,128)(2,1)S(1)}, f32[256,1024]{1,0:T(8,128)S(1)}, f32[256,1]{1,0:T(8,128)S(1)}, bf16[1024,512]{1,0:T(8,128)(2,1)S(1)}) custom-call(s32[1]{0:T(128)S(6)} %copy.11.count_ref, bf16[256,1024]{1,0:T(8,128)(2,1)} %x_hbm.1, bf16[256,512]{1,0:T(8,128)(2,1)} %cot_hbm.1, ...), custom_call_target="tpu_custom_call" | custom-call | flops 5242880 | bytes 3000000 | tf_op jit(solution)/shard_map/prepare/pallas_call | solution.py:293
  3.0 0.0 copy-start
  3.0 8.8 %collective-permute-start = (bf16[256,1024]{1,0:T(8,128)(2,1)S(1)}, bf16[256,1024]{1,0:T(8,128)(2,1)S(1)}, u32[]{:S(2)}, u32[]{:S(2)}) collective-permute-start(bf16[256,1024]{1,0:T(8,128)(2,1)S(1)} %get-tuple-element.20.send_ref), channel_id=1, source_target_pairs={{0,1},{1,0},{2,3},{3,2},{4,5},{5,4},{6,7},{7,6},{8,9},{9,8},{10,11... | collective-permute-start | bytes 1572872 | tf_op jit(solution)/shard_map/ppermute | solution.py:315
  11.8 0.0 copy-done
  11.8 1.5 %own.1 = (f32[512,512]{1,0:T(8,128)S(1)}, f32[16,128]{1,0:T(8,128)S(1)}, bf16[256,1024]{1,0:T(8,128)(2,1)}) custom-call(s32[1]{0:T(128)S(6)} %copy.11.count_ref, bf16[256,512]{1,0:T(8,128)(2,1)S(1)} %get-tuple-element.17.hidden_ref, f32[256,1024]{1,0:T(8,128)S(1)} %get-tuple-element.18.normed_ref, f32[256,1]{1,0:T(8,128)S(1)} %get-tuple-element.19.inv_std_ref, ...), custom_call_target="tpu_custom_call" | custom-call | flops 402653184 | bytes 3000000 | tf_op jit(solution)/shard_map/own/pallas_call | solution.py:316
  13.2 0.0 collective-permute-done.got_ref
  13.3 0.4 pair.1
  13.7 13.2 %all_to_all.10.got_ref = bf16[16,144,128]{2,1,0:T(8,128)(2,1)S(1)} all-to-all(bf16[16,144,128]{2,1,0:T(8,128)(2,1)S(1)} %pair.1), channel_id=1, replica_groups={{11,0,1,2,3,4,5,6,7,8,9,10,12,13,14,15},{27,16,17,18,19,20,21,22,23,24,..., dimensions={0} | all-to-all | bytes 1179648 | tf_op jit(solution)/shard_map/all_to_all | solution.py:275
  26.9 0.2 regroup.1
  27.1 18.3 %all_to_all.11.got_ref = bf16[32,24,128]{2,1,0:T(8,128)(2,1)S(1)} all-to-all(bf16[32,24,128]{2,1,0:T(8,128)(2,1)S(1)} %regroup.1), channel_id=1, replica_groups={{288,0,16,32,48,64,80,96,112,128,144,160,176,192,208,224,240,256,272,30..., dimensions={0} | all-to-all | bytes 393216 | tf_op jit(solution)/shard_map/all_to_all | solution.py:275
  45.3 1.0 %finish.1 = (f32[2,512]{1,0:T(2,128)}, f32[1,1024]{1,0:T(1,128)}, f32[1,1024]{1,0:T(1,128)}, f32[1,512]{1,0:T(1,128)}) custom-call(bf16[32,24,128]{2,1,0:T(8,128)(2,1)S(1)} %all_to_all.11.got_ref, bf16[1024,512]{1,0:T(8,128)(2,1)S(1)} %get-tuple-element.21.weight_ref.projection_ref), custom_call_target="tpu_custom_call" | custom-call | flops 1000000 | bytes 300000 | tf_op jit(solution)/shard_map/finish/pallas_call | solution.py:356
Async XLA Ops:
  3.0 8.8 %copy-start = (f32[1024]{0:T(1024)S(1)}, f32[1024]{0:T(1024)}, u32[]{:S(2)}) copy-start(f32[1024]{0:T(1024)} %param.10) | copy-start | bytes 12292
  3.0 10.3 %collective-permute-start = (bf16[256,1024]{1,0:T(8,128)(2,1)S(1)}, bf16[256,1024]{1,0:T(8,128)(2,1)S(1)}, u32[]{:S(2)}, u32[]{:S(2)}) collective-permute-start(bf16[256,1024]{1,0:T(8,128)(2,1)S(1)} %get-tuple-element.20.send_ref), channel_id=1, source_target_pairs={{0,1},{1,0},{2,3},{3,2},{4,5},{5,4},{6,7},{7,6},{8,9},{9,8},{10,11... | collective-permute-start | bytes 1572872 | tf_op jit(solution)/shard_map/ppermute | solution.py:315
